TPU v7x, 32 devices: a whole 2x2x4 slice. The times are simulated.
32 devices in a mesh: grp: 2 (over y), gx: 4 (over x, core), gy: 4 (over z).
Axes of the slice: x: 2, y: 2, z: 4, core: 2. Of those that a mesh axis runs over, the one named last changes fastest.
Arguments:
- permeability: float32 [8192, 512], P(('grp', 'gx'), 'gy'), parts along dimension 0, may hold values from 0.01 to 100
- support: int32 [256, 16, 36], P(('grp', 'gx'), 'gy'), parts along dimension 0, may hold values 0 or 1
Outputs:
- basis: float32 [256, 16, 36, 256], P(('grp', 'gx'), 'gy'), parts along dimension 0
There are 2 independent parts, one for each index of `grp`. A program takes and returns all parts, laid end to end along the dimension named above; each array names one. Nothing has to cross between parts.
Inputs may be any that keep to these rules, and one draw needn't show every extreme that they name: 0 or 1 for each tile of the 6 x 6 around a block; the block's own 2 x 2 tiles are in the support whatever their entry.
All inputs are finite; a program needn't handle non-finite values.
Results may differ from a plain program's by a relative error of at most 0.00002.
Values sent between devices are 32-bit elements; how exact they have to be, the bound alone decides.
No kernel may reach another device: no remote copies, remote signals or barrier semaphores. Data moves between devices by JAX's collectives and lax.ppermute only.
A program may use at most 192 MiB of HBM per device.

v0:
```python
import jax
import jax.numpy as jnp
from jax import lax
from jax.sharding import PartitionSpec as P

ITERS = 4


OMEGA = 2.0 / 3.0


def from_behind(value, axis, by):
    devices = lax.axis_size(axis)
    pairs = [(i, i + by) for i in range(devices) if 0 <= i + by < devices]
    return lax.ppermute(value, axis, pairs)


def with_halo(block, sides, width):
    for axis, dim in sides:
        count = lax.axis_size(axis)
        forward = [(i, i + 1) for i in range(count - 1)]
        backward = [(target, source) for source, target in forward]
        low = lax.ppermute(
            lax.slice_in_dim(block, block.shape[dim] - width, None, axis=dim), axis, forward
        )
        high = lax.ppermute(lax.slice_in_dim(block, 0, width, axis=dim), axis, backward)
        block = jnp.concatenate([low, block, high], axis=dim)
    return block


def face_fields(haloed, first_x, first_y, grid_rows, grid_cols):
    rows_h, cols_h = haloed.shape
    coord_x = first_x - 33 + jnp.arange(rows_h, dtype=jnp.int32)
    coord_y = first_y - 33 + jnp.arange(cols_h, dtype=jnp.int32)
    inside = ((coord_x >= 0) & (coord_x < grid_rows))[:, None] & (
        (coord_y >= 0) & (coord_y < grid_cols)
    )[None, :]
    perm = jnp.where(inside, haloed, jnp.float32(1.0))
    both_x = inside[:-1] & inside[1:]
    face_x = jnp.where(
        both_x, 2.0 * perm[:-1] * perm[1:] / (perm[:-1] + perm[1:]), jnp.float32(0.0)
    )
    both_y = inside[:, :-1] & inside[:, 1:]
    face_y = jnp.where(
        both_y, 2.0 * perm[:, :-1] * perm[:, 1:] / (perm[:, :-1] + perm[:, 1:]), jnp.float32(0.0)
    )
    west = face_x[:-1, 1:-1]
    east = face_x[1:, 1:-1]
    south = face_y[1:-1, :-1]
    north = face_y[1:-1, 1:]
    inside_ext = inside[1:-1, 1:-1]
    diag = jnp.where(inside_ext, west + east + south + north, jnp.float32(1.0))
    return (west, east, south, north, diag, inside_ext)


def by_offset(field, rows, cols):
    return jnp.stack(
        [
            jnp.stack([field[32 * r : 32 * r + rows, 32 * c : 32 * c + cols] for c in range(3)])
            for r in range(3)
        ]
    )


def piece_masks(support, inside_off, rows, cols):
    blocks_x, blocks_y = (support.shape[0], support.shape[1])
    offsets = jnp.arange(3, dtype=jnp.int32)
    own_row = offsets == 1
    own_pair = own_row[:, None] & own_row[None, :]
    tiles = support.reshape(blocks_x, blocks_y, 3, 2, 3, 2) == 1
    tiles = tiles.transpose(2, 4, 0, 3, 1, 5) | own_pair[:, :, None, None, None, None]
    wide = jnp.broadcast_to(
        tiles[:, :, :, :, None, :, :, None], (3, 3, blocks_x, 2, 16, blocks_y, 2, 16)
    )
    cell_mask = wide.reshape(3, 3, rows, cols) & inside_off
    own_cells = own_pair[:, :, None, None] & inside_off
    return (cell_mask, own_cells)


def smooth_pieces(values, west, east, south, north, diag, cell_mask):
    rows, cols = (values.shape[2], values.shape[3])
    pos_x = (jnp.arange(rows, dtype=jnp.int32) % 32)[None, None, :, None]
    pos_y = (jnp.arange(cols, dtype=jnp.int32) % 32)[None, None, None, :]
    same_w = jnp.pad(values, ((0, 0), (0, 0), (1, 0), (0, 0)))[:, :, :rows, :]
    cross_w = jnp.pad(values, ((1, 0), (0, 0), (0, 31), (0, 0)))[:3, :, 31:, :]
    from_west = jnp.where(pos_x == 0, cross_w, same_w)
    same_e = jnp.pad(values, ((0, 0), (0, 0), (0, 1), (0, 0)))[:, :, 1:, :]
    cross_e = jnp.pad(values, ((0, 1), (0, 0), (31, 0), (0, 0)))[1:, :, :rows, :]
    from_east = jnp.where(pos_x == 31, cross_e, same_e)
    same_s = jnp.pad(values, ((0, 0), (0, 0), (0, 0), (1, 0)))[:, :, :, :cols]
    cross_s = jnp.pad(values, ((0, 0), (1, 0), (0, 0), (0, 31)))[:, :3, :, 31:]
    from_south = jnp.where(pos_y == 0, cross_s, same_s)
    same_n = jnp.pad(values, ((0, 0), (0, 0), (0, 0), (0, 1)))[:, :, :, 1:]
    cross_n = jnp.pad(values, ((0, 0), (0, 1), (0, 0), (31, 0)))[:, 1:, :, :cols]
    from_north = jnp.where(pos_y == 31, cross_n, same_n)
    beside = west * from_west + east * from_east + south * from_south + north * from_north
    return jnp.where(cell_mask, (1.0 - OMEGA) * values + OMEGA * beside / diag, jnp.float32(0.0))


def assemble_pieces(smoothed):
    rows, cols = (smoothed.shape[2], smoothed.shape[3])
    total = jnp.zeros((rows + 64, cols + 64), jnp.float32)
    for row_off in range(3):
        for col_off in range(3):
            total = total + jnp.pad(
                smoothed[row_off, col_off],
                ((32 * row_off, 64 - 32 * row_off), (32 * col_off, 64 - 32 * col_off)),
            )
    return total


def pieces_to_tiles(values):
    rows, cols = (values.shape[2], values.shape[3])
    blocks_x, blocks_y = (rows // 32, cols // 32)
    split = values.reshape(3, 3, blocks_x, 2, 16, blocks_y, 2, 16).transpose(2, 5, 0, 3, 1, 6, 4, 7)
    return split.reshape(blocks_x, blocks_y, 36, 256)


def pass_along_x(strip, offset):
    return from_behind(strip, "gx", offset)


def pass_along_y(strip, offset):
    return from_behind(strip, "gy", offset)


def sectioned_totals(extended):
    from_east = pass_along_x(extended[:32], -1)
    from_west = pass_along_x(extended[-32:], 1)
    middle = extended[32:-32]
    middle = middle.at[:32].add(from_west)
    middle = middle.at[-32:].add(from_east)
    from_north = pass_along_y(middle[:, :32], -1)
    from_south = pass_along_y(middle[:, -32:], 1)
    totals = middle[:, 32:-32]
    totals = totals.at[:, :32].add(from_south)
    totals = totals.at[:, -32:].add(from_north)
    return with_halo(totals, (("gx", 0), ("gy", 1)), 32)


def body(permeability, support):
    rows, cols = permeability.shape
    first_x = lax.axis_index("gx") * rows
    first_y = lax.axis_index("gy") * cols
    grid_rows = rows * lax.axis_size("gx")
    grid_cols = cols * lax.axis_size("gy")
    haloed = with_halo(permeability, (("gx", 0), ("gy", 1)), 33)
    west, east, south, north, diag, inside_ext = face_fields(
        haloed, first_x, first_y, grid_rows, grid_cols
    )
    west_p, east_p, south_p, north_p, diag_p = [
        by_offset(field, rows, cols) for field in (west, east, south, north, diag)
    ]
    inside_off = by_offset(inside_ext, rows, cols)
    cell_mask, own_cells = piece_masks(support, inside_off, rows, cols)
    start = jnp.where(own_cells, jnp.float32(1.0), jnp.float32(0.0))

    def iterate(count, values):
        smoothed = smooth_pieces(values, west_p, east_p, south_p, north_p, diag_p, cell_mask)
        extended = assemble_pieces(smoothed)
        beside_all = sectioned_totals(extended)
        back = by_offset(beside_all, rows, cols)
        return smoothed / jnp.where(inside_off, back, jnp.float32(1.0))

    final = lax.fori_loop(0, ITERS, iterate, start)
    return pieces_to_tiles(final)


def solution(mesh):
    return jax.shard_map(
        body,
        mesh=mesh,
        in_specs=(P(("grp", "gx"), "gy"), P(("grp", "gx"), "gy", None)),
        out_specs=P(("grp", "gx"), "gy", None, None),
        check_vma=False,
    )
```

profile of v0, /device:TPU:1, one launch (start us, length us, event | category | flops | bytes accessed | tf_op | source)
XLA Modules:
  0.0 570.4 jit_solution(7927562465349626723)
XLA Ops:
  0.8 2.0 collective-permute-start.9
  2.7 4.5 collective-permute-start.8
  10.5 13.9 %broadcast_in_dim.111 = pred[3,3,32,2,16,4,2,16]{7,6,5,4,3,2,1,0:T(4,128)(4,1)} broadcast(pred[3,3,32,2,4,2]{5,4,3,2,1,0:T(4,128)(4,1)S(1)} %copy.14), dimensions={0,1,2,3,5,6} | broadcast | bytes 1184256 | tf_op jit(solution)/shard_map/broadcast_in_dim | solution.py:72
  24.3 47.5 %reshape.218 = pred[3,3,1024,128]{3,2,1,0:T(8,128)(4,1)S(1)} reshape(pred[3,3,32,2,16,4,2,16]{7,6,5,4,3,2,1,0:T(4,128)(4,1)} %broadcast_in_dim.111) | data formatting | bytes 2359296 | tf_op jit(solution)/shard_map/reshape | solution.py:75
  73.8 2.1 concatenate.71
  79.1 2.0 copy.10
  82.3 4.7 collective-permute-start.10
  87.0 3.9 and_select_fusion.1
  90.9 6.1 %copy.15 = f32[3,3,1024,128]{2,3,1,0:T(8,128)} copy(f32[3,3,1024,128]{3,2,1,0:T(8,128)} %and_select_fusion.1) | data formatting | bytes 9437184 | tf_op jit(solution)/shard_map/while | solution.py:165
  96.9 2.5 copy.22
  107.1 6.1 %slice_bitcast_fusion.44 = (f32[1,1024,128]{2,1,0:T(8,128)}, f32[1,1024,128]{2,1,0:T(8,128)}, f32[1,1024,128]{2,1,0:T(8,128)}, f32[1,1024,128]{2,1,0:T(8,128)}, ...) fusion(f32[1089,194]{1,0:T(8,128)S(1)} %divide_select_fusion.1), kind=kLoop, calls=%fused_computation.149 | loop fusion | bytes 18874368 | tf_op jit(solution)/shard_map/stack | solution.py:59
  113.3 3.2 fusion.35
  116.5 5.7 %slice_bitcast_fusion.26 = (f32[1,1024,128]{2,1,0:T(8,128)}, f32[1,1024,128]{2,1,0:T(8,128)}, f32[1,1024,128]{2,1,0:T(8,128)}, f32[1,1024,128]{2,1,0:T(8,128)}, ...) fusion(f32[1090,193]{1,0:T(8,128)S(1)} %divide_select_fusion), kind=kLoop, calls=%fused_computation.131 | loop fusion | bytes 18874368 | tf_op jit(solution)/shard_map/stack | solution.py:59
  123.4 2.5 pad_maximum_fusion.8
  125.9 6.1 %copy.20 = f32[3,3,1024,128]{2,3,1,0:T(8,128)} copy(f32[3,3,1024,128]{3,2,1,0:T(8,128)} %pad_maximum_fusion.8) | data formatting | bytes 9437184 | tf_op jit(solution)/shard_map/while | solution.py:165
  132.1 2.2 maximum_bitcast_fusion.5
  135.0 2.5 pad_maximum_fusion.5
  137.5 6.1 %copy.17 = f32[3,3,1024,128]{2,3,1,0:T(8,128)} copy(f32[3,3,1024,128]{3,2,1,0:T(8,128)} %pad_maximum_fusion.5) | data formatting | bytes 9437184 | tf_op jit(solution)/shard_map/while | solution.py:165
  145.5 2.5 pad_maximum_fusion.4
  148.0 6.0 %copy.16 = f32[3,3,1024,128]{2,3,1,0:T(8,128)} copy(f32[3,3,1024,128]{3,2,1,0:T(8,128)} %pad_maximum_fusion.4) | data formatting | bytes 9437184 | tf_op jit(solution)/shard_map/while | solution.py:165
  154.1 2.2 maximum_bitcast_fusion.11
  157.1 2.5 pad_maximum_fusion.7
  159.6 6.1 %copy.19 = f32[3,3,1024,128]{2,3,1,0:T(8,128)} copy(f32[3,3,1024,128]{3,2,1,0:T(8,128)} %pad_maximum_fusion.7) | data formatting | bytes 9437184 | tf_op jit(solution)/shard_map/while | solution.py:165
  167.6 2.5 pad_maximum_fusion.6
  170.1 6.0 %copy.18 = f32[3,3,1024,128]{2,3,1,0:T(8,128)} copy(f32[3,3,1024,128]{3,2,1,0:T(8,128)} %pad_maximum_fusion.6) | data formatting | bytes 9437184 | tf_op jit(solution)/shard_map/while | solution.py:165
  176.1 271.0 %while.18 = (s32[]{:T(128)}, f32[3,3,1024,128]{2,3,1,0:T(8,128)}, f32[3,3,1024,128]{2,3,1,0:T(8,128)}, f32[3,3,1024,128]{2,3,1,0:T(8,128)}, f32[3,3,1024,128]{2,...) while((s32[]{:T(128)}, f32[3,3,1024,128]{2,3,1,0:T(8,128)}, ...), condition=%wide.region_3.4_spmd, body=%wide.region_1.3_spmd.sunk | while | flops 28824580 | bytes 125817904 | solution.py:165
  176.1 22.1 %fusion.58 = f32[3,3,1024,128]{2,3,1,0:T(8,128)S(1)} fusion(pred[3,3,1024,128]{2,3,1,0:T(8,128)(4,1)S(1)} %get-tuple-element.573, f32[3,3,1024,128]{2,3,1,0:T(8,128)} %get-tuple-element.572, f32[3,3,1024,128]{2,3,1,0:T(8,128)} %get-tuple-element.570, f32[3,3,1024,128]{2,3,1,0:T(8,128)} %get-tuple-element.554, ...), kind=kLoop, calls=%fused_computation.15.clone.1 | loop fusion | flops 18874368 | bytes 34212096 | tf_op jit(solution)/shard_map/while/body/eval_jaxpr/jit(_where)/select_n | solution.py:97
  201.5 3.0 collective-permute-start
  207.7 2.7 collective-permute-done.1
  211.3 2.6 collective-permute-start.2
  216.5 4.2 collective-permute-done.3
  221.5 3.0 collective-permute-start.4
  226.4 3.6 collective-permute-done.5
  230.4 3.6 collective-permute-start.6
  236.1 3.8 collective-permute-done.7
  243.2 2.8 fusion.67
  246.0 22.1 %fusion.58 = f32[3,3,1024,128]{2,3,1,0:T(8,128)S(1)} fusion(pred[3,3,1024,128]{2,3,1,0:T(8,128)(4,1)S(1)} %get-tuple-element.573, f32[3,3,1024,128]{2,3,1,0:T(8,128)} %get-tuple-element.572, f32[3,3,1024,128]{2,3,1,0:T(8,128)} %get-tuple-element.570, f32[3,3,1024,128]{2,3,1,0:T(8,128)} %get-tuple-element.554, ...), kind=kLoop, calls=%fused_computation.15.clone.1 | loop fusion | flops 18874368 | bytes 34212096 | tf_op jit(solution)/shard_map/while/body/eval_jaxpr/jit(_where)/select_n | solution.py:97
  271.4 3.3 collective-permute-start
  277.9 2.7 collective-permute-done.1
  285.8 3.7 collective-permute-done.3
  290.3 3.2 collective-permute-start.4
  295.4 3.6 collective-permute-done.5
  303.2 3.8 collective-permute-done.7
  310.3 2.8 fusion.67
  313.0 22.1 %fusion.58 = f32[3,3,1024,128]{2,3,1,0:T(8,128)S(1)} fusion(pred[3,3,1024,128]{2,3,1,0:T(8,128)(4,1)S(1)} %get-tuple-element.573, f32[3,3,1024,128]{2,3,1,0:T(8,128)} %get-tuple-element.572, f32[3,3,1024,128]{2,3,1,0:T(8,128)} %get-tuple-element.570, f32[3,3,1024,128]{2,3,1,0:T(8,128)} %get-tuple-element.554, ...), kind=kLoop, calls=%fused_computation.15.clone.1 | loop fusion | flops 18874368 | bytes 34212096 | tf_op jit(solution)/shard_map/while/body/eval_jaxpr/jit(_where)/select_n | solution.py:97
  338.4 3.3 collective-permute-start
  344.9 2.7 collective-permute-done.1
  352.9 3.7 collective-permute-done.3
  357.3 3.2 collective-permute-start.4
  362.5 3.6 collective-permute-done.5
  370.2 3.8 collective-permute-done.7
  377.3 2.8 fusion.67
  380.1 22.1 %fusion.58 = f32[3,3,1024,128]{2,3,1,0:T(8,128)S(1)} fusion(pred[3,3,1024,128]{2,3,1,0:T(8,128)(4,1)S(1)} %get-tuple-element.573, f32[3,3,1024,128]{2,3,1,0:T(8,128)} %get-tuple-element.572, f32[3,3,1024,128]{2,3,1,0:T(8,128)} %get-tuple-element.570, f32[3,3,1024,128]{2,3,1,0:T(8,128)} %get-tuple-element.554, ...), kind=kLoop, calls=%fused_computation.15.clone.1 | loop fusion | flops 18874368 | bytes 34212096 | tf_op jit(solution)/shard_map/while/body/eval_jaxpr/jit(_where)/select_n | solution.py:97
  405.5 3.3 collective-permute-start
  412.0 2.7 collective-permute-done.1
  419.9 3.7 collective-permute-done.3
  424.4 3.2 collective-permute-start.4
  429.6 3.6 collective-permute-done.5
  437.3 3.8 collective-permute-done.7
  444.4 2.8 fusion.67
  447.1 6.0 %copy.23 = f32[3,3,1024,128]{3,2,1,0:T(8,128)} copy(f32[3,3,1024,128]{2,3,1,0:T(8,128)} %get-tuple-element.282) | data formatting | bytes 9437184 | tf_op jit(solution)/shard_map/while | solution.py:165
  453.2 55.2 %reshape.219 = f32[3,3,32,2,16,4,2,16]{7,6,5,4,3,2,1,0:T(2,128)} reshape(f32[3,3,1024,128]{3,2,1,0:T(8,128)} %copy.23) | data formatting | bytes 9437184 | tf_op jit(solution)/shard_map/reshape | solution.py:115
  508.4 48.4 %copy.24 = f32[32,4,3,2,3,2,16,16]{0,7,6,5,4,3,2,1:T(8,128)} copy(f32[32,4,3,2,3,2,16,16]{7,5,1,6,3,0,4,2:T(2,128)} %bitcast.209) | data formatting | bytes 9437184 | tf_op jit(solution)/shard_map/transpose | solution.py:115
  556.7 13.6 %copy.25 = f32[32,4,36,256]{3,1,2,0:T(4,128)} copy(f32[32,4,36,256]{0,3,2,1:T(8,128)} %bitcast.210) | data formatting | bytes 9437184 | tf_op jit(solution)/shard_map/reshape | solution.py:116
  (241 shorter events, 107.1 us)
Async XLA Ops:
  0.8 73.0 %collective-permute-start.9 = (f32[33,128]{1,0:T(8,128)S(1)}, f32[33,128]{1,0:T(8,128)S(1)}, u32[]{:S(2)}, u32[]{:S(2)}) collective-permute-start(f32[33,128]{1,0:T(8,128)S(1)} %get-tuple-element.394), channel_id=1, source_target_pairs={{4,0},{8,4},{12,8},{5,1},{9,5},{13,9},{6,2},{10,6},{14,10},{7,3},{... | collective-permute-start | bytes 50696 | tf_op jit(solution)/shard_map/ppermute | solution.py:26
  2.7 71.1 %collective-permute-start.8 = (f32[33,128]{1,0:T(8,128)S(1)}, f32[33,128]{1,0:T(8,128)S(1)}, u32[]{:S(2)}, u32[]{:S(2)}) collective-permute-start(f32[33,128]{1,0:T(8,128)S(1)} %get-tuple-element.395), channel_id=1, source_target_pairs={{0,4},{4,8},{8,12},{1,5},{5,9},{9,13},{2,6},{6,10},{10,14},{3,7},{... | collective-permute-start | bytes 50696 | tf_op jit(solution)/shard_map/ppermute | solution.py:23
  9.2 95.8 %copy-start.3 = (pred[1090,194]{1,0:T(8,128)(4,1)}, pred[1090,194]{1,0:T(8,128)(4,1)S(1)}, u32[]{:S(2)}) copy-start(pred[1090,194]{1,0:T(8,128)(4,1)S(1)} %broadcast_and_fusion) | copy-start | bytes 634384
  76.0 11.0 %copy-start.6 = (pred[1,3,1024,128]{3,2,1,0:T(8,128)(4,1)S(1)}, pred[1,3,1024,128]{3,2,1,0:T(8,128)(4,1)}, u32[]{:S(2)}) copy-start(pred[1,3,1024,128]{3,2,1,0:T(8,128)(4,1)} %copy-done.5) | copy-start | bytes 1179652
  81.0 22.1 %collective-permute-start.11 = (f32[1090,33]{0,1:T(8,128)}, f32[1090,33]{0,1:T(8,128)}, u32[]{:S(2)}, u32[]{:S(2)}) collective-permute-start(f32[1090,33]{0,1:T(8,128)} %copy.10), channel_id=1, source_target_pairs={{1,0},{2,1},{3,2},{5,4},{6,5},{7,6},{9,8},{10,9},{11,10},{13,12},{... | collective-permute-start | bytes 431648 | tf_op jit(solution)/shard_map/ppermute | solution.py:26
  82.3 19.7 %collective-permute-start.10 = (f32[1090,33]{0,1:T(8,128)}, f32[1090,33]{0,1:T(8,128)}, u32[]{:S(2)}, u32[]{:S(2)}) collective-permute-start(f32[1090,33]{0,1:T(8,128)} %copy.9), channel_id=1, source_target_pairs={{0,1},{1,2},{2,3},{4,5},{5,6},{6,7},{8,9},{9,10},{10,11},{12,13},{... | collective-permute-start | bytes 431648 | tf_op jit(solution)/shard_map/ppermute | solution.py:23
  96.9 2.5 copy-start.4
  116.5 5.7 %copy-start.2 = (f32[1088,192]{1,0:T(8,128)S(1)}, f32[1088,192]{1,0:T(8,128)}, u32[]{:S(2)}) copy-start(f32[1088,192]{1,0:T(8,128)} %fusion.35) | copy-start | bytes 2506756
  132.0 2.2 copy-start.16
  132.0 2.2 copy-start.17
  132.0 2.3 copy-start.18
  132.0 2.5 copy-start.19
  132.0 2.6 copy-start.20
  132.0 2.8 copy-start.21
  137.5 6.1 %copy-start.15 = (f32[1,1024,128]{2,1,0:T(8,128)S(1)}, f32[1,1024,128]{2,1,0:T(8,128)}, u32[]{:S(2)}) copy-start(f32[1,1024,128]{2,1,0:T(8,128)} %get-tuple-element.377) | copy-start | bytes 1572868
  154.1 2.2 copy-start.9
  154.1 2.2 copy-start.10
  154.1 2.3 copy-start.11
  154.1 2.5 copy-start.12
  154.1 2.6 copy-start.13
  154.1 2.8 copy-start.14
  159.6 6.1 %copy-start.8 = (f32[1,1024,128]{2,1,0:T(8,128)S(1)}, f32[1,1024,128]{2,1,0:T(8,128)}, u32[]{:S(2)}) copy-start(f32[1,1024,128]{2,1,0:T(8,128)} %get-tuple-element.359) | copy-start | bytes 1572868
  198.2 2.2 copy-start
  201.5 5.2 collective-permute-start
  204.5 5.9 %collective-permute-start.1 = (f32[32,192]{0,1:T(8,128)S(1)}, f32[32,192]{0,1:T(8,128)S(1)}, u32[]{:S(2)}, u32[]{:S(2)}) collective-permute-start(f32[32,192]{0,1:T(8,128)S(1)} %get-tuple-element.525), channel_id=1, source_target_pairs={{4,0},{8,4},{12,8},{5,1},{9,5},{13,9},{6,2},{10,6},{14,10},{7,3},{... | collective-permute-start | bytes 73736 | tf_op jit(solution)/shard_map/while/body/eval_jaxpr/ppermute | solution.py:15
  211.3 4.6 collective-permute-start.2
  214.6 6.2 %collective-permute-start.3 = (f32[1024,32]{0,1:T(8,128)S(1)}, f32[1024,32]{0,1:T(8,128)S(1)}, u32[]{:S(2)}, u32[]{:S(2)}) collective-permute-start(f32[1024,32]{0,1:T(8,128)S(1)} %get-tuple-element.527), channel_id=1, source_target_pairs={{1,0},{2,1},{3,2},{5,4},{6,5},{7,6},{9,8},{10,9},{11,10},{13,12},{... | collective-permute-start | bytes 393224 | tf_op jit(solution)/shard_map/while/body/eval_jaxpr/ppermute | solution.py:15
  221.5 4.9 collective-permute-start.4
  224.5 5.6 collective-permute-start.5
  230.4 5.7 %collective-permute-start.6 = (f32[1088,32]{0,1:T(8,128)S(1)}, f32[1088,32]{0,1:T(8,128)S(1)}, u32[]{:S(2)}, u32[]{:S(2)}) collective-permute-start(f32[1088,32]{0,1:T(8,128)S(1)} %get-tuple-element.530), channel_id=1, source_target_pairs={{0,1},{1,2},{2,3},{4,5},{5,6},{6,7},{8,9},{9,10},{10,11},{12,13},{... | collective-permute-start | bytes 417800 | tf_op jit(solution)/shard_map/while/body/eval_jaxpr/ppermute | solution.py:23
  234.1 5.9 %collective-permute-start.7 = (f32[1088,32]{0,1:T(8,128)S(1)}, f32[1088,32]{0,1:T(8,128)S(1)}, u32[]{:S(2)}, u32[]{:S(2)}) collective-permute-start(f32[1088,32]{0,1:T(8,128)S(1)} %get-tuple-element.531), channel_id=1, source_target_pairs={{1,0},{2,1},{3,2},{5,4},{6,5},{7,6},{9,8},{10,9},{11,10},{13,12},{... | collective-permute-start | bytes 417800 | tf_op jit(solution)/shard_map/while/body/eval_jaxpr/ppermute | solution.py:26
  240.6 2.2 slice-start.1
  240.9 2.3 copy-start.1
  268.1 2.2 copy-start
  271.4 5.5 collective-permute-start
  274.7 5.9 %collective-permute-start.1 = (f32[32,192]{0,1:T(8,128)S(1)}, f32[32,192]{0,1:T(8,128)S(1)}, u32[]{:S(2)}, u32[]{:S(2)}) collective-permute-start(f32[32,192]{0,1:T(8,128)S(1)} %get-tuple-element.525), channel_id=1, source_target_pairs={{4,0},{8,4},{12,8},{5,1},{9,5},{13,9},{6,2},{10,6},{14,10},{7,3},{... | collective-permute-start | bytes 73736 | tf_op jit(solution)/shard_map/while/body/eval_jaxpr/ppermute | solution.py:15
  281.5 3.7 collective-permute-start.2
  283.8 5.7 %collective-permute-start.3 = (f32[1024,32]{0,1:T(8,128)S(1)}, f32[1024,32]{0,1:T(8,128)S(1)}, u32[]{:S(2)}, u32[]{:S(2)}) collective-permute-start(f32[1024,32]{0,1:T(8,128)S(1)} %get-tuple-element.527), channel_id=1, source_target_pairs={{1,0},{2,1},{3,2},{5,4},{6,5},{7,6},{9,8},{10,9},{11,10},{13,12},{... | collective-permute-start | bytes 393224 | tf_op jit(solution)/shard_map/while/body/eval_jaxpr/ppermute | solution.py:15
  290.3 5.2 collective-permute-start.4
  293.5 5.6 collective-permute-start.5
  299.5 3.7 collective-permute-start.6
  301.1 5.9 %collective-permute-start.7 = (f32[1088,32]{0,1:T(8,128)S(1)}, f32[1088,32]{0,1:T(8,128)S(1)}, u32[]{:S(2)}, u32[]{:S(2)}) collective-permute-start(f32[1088,32]{0,1:T(8,128)S(1)} %get-tuple-element.531), channel_id=1, source_target_pairs={{1,0},{2,1},{3,2},{5,4},{6,5},{7,6},{9,8},{10,9},{11,10},{13,12},{... | collective-permute-start | bytes 417800 | tf_op jit(solution)/shard_map/while/body/eval_jaxpr/ppermute | solution.py:26
  307.6 2.2 slice-start.1
  308.0 2.3 copy-start.1
  338.4 5.5 collective-permute-start
  341.7 5.9 %collective-permute-start.1 = (f32[32,192]{0,1:T(8,128)S(1)}, f32[32,192]{0,1:T(8,128)S(1)}, u32[]{:S(2)}, u32[]{:S(2)}) collective-permute-start(f32[32,192]{0,1:T(8,128)S(1)} %get-tuple-element.525), channel_id=1, source_target_pairs={{4,0},{8,4},{12,8},{5,1},{9,5},{13,9},{6,2},{10,6},{14,10},{7,3},{... | collective-permute-start | bytes 73736 | tf_op jit(solution)/shard_map/while/body/eval_jaxpr/ppermute | solution.py:15
  348.5 3.7 collective-permute-start.2
  350.9 5.7 %collective-permute-start.3 = (f32[1024,32]{0,1:T(8,128)S(1)}, f32[1024,32]{0,1:T(8,128)S(1)}, u32[]{:S(2)}, u32[]{:S(2)}) collective-permute-start(f32[1024,32]{0,1:T(8,128)S(1)} %get-tuple-element.527), channel_id=1, source_target_pairs={{1,0},{2,1},{3,2},{5,4},{6,5},{7,6},{9,8},{10,9},{11,10},{13,12},{... | collective-permute-start | bytes 393224 | tf_op jit(solution)/shard_map/while/body/eval_jaxpr/ppermute | solution.py:15
  357.3 5.2 collective-permute-start.4
  360.6 5.6 collective-permute-start.5
  366.5 3.7 collective-permute-start.6
  368.2 5.9 %collective-permute-start.7 = (f32[1088,32]{0,1:T(8,128)S(1)}, f32[1088,32]{0,1:T(8,128)S(1)}, u32[]{:S(2)}, u32[]{:S(2)}) collective-permute-start(f32[1088,32]{0,1:T(8,128)S(1)} %get-tuple-element.531), channel_id=1, source_target_pairs={{1,0},{2,1},{3,2},{5,4},{6,5},{7,6},{9,8},{10,9},{11,10},{13,12},{... | collective-permute-start | bytes 417800 | tf_op jit(solution)/shard_map/while/body/eval_jaxpr/ppermute | solution.py:26
  374.7 2.2 slice-start.1
  375.0 2.3 copy-start.1
  405.5 5.5 collective-permute-start
  408.8 5.9 %collective-permute-start.1 = (f32[32,192]{0,1:T(8,128)S(1)}, f32[32,192]{0,1:T(8,128)S(1)}, u32[]{:S(2)}, u32[]{:S(2)}) collective-permute-start(f32[32,192]{0,1:T(8,128)S(1)} %get-tuple-element.525), channel_id=1, source_target_pairs={{4,0},{8,4},{12,8},{5,1},{9,5},{13,9},{6,2},{10,6},{14,10},{7,3},{... | collective-permute-start | bytes 73736 | tf_op jit(solution)/shard_map/while/body/eval_jaxpr/ppermute | solution.py:15
  415.6 3.7 collective-permute-start.2
  418.0 5.7 %collective-permute-start.3 = (f32[1024,32]{0,1:T(8,128)S(1)}, f32[1024,32]{0,1:T(8,128)S(1)}, u32[]{:S(2)}, u32[]{:S(2)}) collective-permute-start(f32[1024,32]{0,1:T(8,128)S(1)} %get-tuple-element.527), channel_id=1, source_target_pairs={{1,0},{2,1},{3,2},{5,4},{6,5},{7,6},{9,8},{10,9},{11,10},{13,12},{... | collective-permute-start | bytes 393224 | tf_op jit(solution)/shard_map/while/body/eval_jaxpr/ppermute | solution.py:15
  424.4 5.2 collective-permute-start.4
  427.6 5.6 collective-permute-start.5
  433.6 3.7 collective-permute-start.6
  435.2 5.9 %collective-permute-start.7 = (f32[1088,32]{0,1:T(8,128)S(1)}, f32[1088,32]{0,1:T(8,128)S(1)}, u32[]{:S(2)}, u32[]{:S(2)}) collective-permute-start(f32[1088,32]{0,1:T(8,128)S(1)} %get-tuple-element.531), channel_id=1, source_target_pairs={{1,0},{2,1},{3,2},{5,4},{6,5},{7,6},{9,8},{10,9},{11,10},{13,12},{... | collective-permute-start | bytes 417800 | tf_op jit(solution)/shard_map/while/body/eval_jaxpr/ppermute | solution.py:26
  441.8 2.2 slice-start.1
  442.1 2.3 copy-start.1
  (8 other events, 12.9 us)
where the time goes:
time: 575 us; the launch traced here: 570 us
  local copies, waits for them, and re-layouts  279 us (49%)
  other arithmetic  153 us (27%)
  starting transfers between devices  79.7 us (14%)
  waiting for transfers between devices  57.9 us (10%)
    select_n x4, other arithmetic, smooth_pieces(): jnp.where(cell_mask, (1.0 - OMEGA) * values + OMEGA * beside / diag, jnp....  88.4 us
    reshape x1, local copies, waits for them, and re-layouts, pieces_to_tiles(): values.reshape(3, 3, blocks_x, 2, 16, blocks_y, 2, 16)  55.2 us
    transpose x1, local copies, waits for them, and re-layouts, pieces_to_tiles(): values.reshape(3, 3, blocks_x, 2, 16, blocks_y, 2, 16)  48.4 us
    reshape x1, local copies, waits for them, and re-layouts, piece_masks(): cell_mask = wide.reshape(3, 3, rows, cols) & inside_off  47.5 us
    while x9, local copies, waits for them, and re-layouts, body(): final = lax.fori_loop(0, ITERS, iterate, start)  46.8 us
    ppermute x16, starting transfers between devices, from_behind(): return lax.ppermute(value, axis, pairs)  33.2 us
    ppermute x10, starting transfers between devices, with_halo(): lax.ppermute(lax.slice_in_dim(block, block.shape[dim] - width, None, axis...  30.4 us
    ppermute x10, waiting for transfers between devices, with_halo(): lax.ppermute(lax.slice_in_dim(block, 0, width, axis=dim), axis, backward)  29.8 us
  transfers between devices with their start and end apart: 36, of which 20 were waited for; matrix products, arithmetic and copies ran while one was open for 17% of the time, Pallas kernels for 0%

commit v1 on v0

v1 whole, which is shorter than its diff:
```python
import jax
import jax.numpy as jnp
from jax import lax
from jax.experimental import pallas as pl
from jax.experimental.pallas import tpu as pltpu
from jax.sharding import PartitionSpec as P

ITERS = 4
SIDES = (-1, 0, 1)
TINY = 1e-30

SEGMENTS = 4
CHUNKS = 2
SEG_BLOCKS = 9
SEG_ROWS = 32 * SEG_BLOCKS
RIM = 8
HALO = 40
PITCH = 304
FIRST, LAST = RIM - (ITERS - 1), RIM + SEG_ROWS + (ITERS - 1)
SUP_PITCH = 40

f32 = jnp.float32


def lanes():
    return lax.broadcasted_iota(jnp.int32, (8, 128), 1)


def window_lane(label):
    lane = lanes()
    return lax.rem(lane + (80 - 32 * label), 96) // 16


def pack_kernel(perm_ref, sup_ref, up_ref, down_ref):
    rows = perm_ref.shape[0]
    half = rows // 2
    low = perm_ref[:half, :]
    high = perm_ref[half:, :]
    left = lax.broadcasted_iota(jnp.int32, (half, 128), 1) < 64
    up_ref[:half, :] = jnp.where(left, pltpu.roll(low, 64, 1), high)
    down_ref[:half, :] = jnp.where(left, low, pltpu.roll(high, 64, 1))
    blocks = sup_ref.shape[0]
    pad = jnp.zeros((blocks, 92), f32)
    wide = [
        jnp.concatenate([sup_ref[:, q, :].astype(f32), pad], axis=1) for q in range(4)
    ]
    up_ref[half:, :] = wide[1] + pltpu.roll(wide[2], 36, 1) + pltpu.roll(wide[3], 72, 1)
    down_ref[half:, :] = wide[0] + pltpu.roll(wide[1], 36, 1) + pltpu.roll(wide[2], 72, 1)


def pack(perm, support):
    rows = perm.shape[0]
    shape = jax.ShapeDtypeStruct((rows // 2 + support.shape[0], 128), f32)
    return pl.pallas_call(pack_kernel, out_shape=(shape, shape), name="pack")(perm, support)


def widen_kernel(perm_ref, sup_ref, left_ref, right_ref, field_ref, wide_ref, up_ref, down_ref):
    rows = perm_ref.shape[0]
    half = rows // 2
    lane = lax.broadcasted_iota(jnp.int32, (half, 128), 1)
    for part in range(2):
        own = perm_ref[part * half : (part + 1) * half, :]
        left = pltpu.roll(left_ref[:half, :], 112 if part == 0 else 48, 1)
        right = pltpu.roll(right_ref[:half, :], 80 if part == 0 else 16, 1)
        field_ref[0, part * half : (part + 1) * half, :] = jnp.where(
            lane < 48, left, pltpu.roll(own, 48, 1)
        )
        field_ref[1, part * half : (part + 1) * half, :] = jnp.where(
            lane < 80, pltpu.roll(own, 80, 1), right
        )
    for chunk in range(2):
        up_ref[chunk * HALO : (chunk + 1) * HALO, :] = field_ref[chunk, rows - HALO :, :]
        down_ref[chunk * HALO : (chunk + 1) * HALO, :] = field_ref[chunk, :HALO, :]
    blocks = sup_ref.shape[0]
    keep = lax.broadcasted_iota(jnp.int32, (blocks, 128), 1) < 36
    pad = jnp.zeros((blocks, 92), f32)
    for q in range(3):
        for source, place in ((left_ref, q), (right_ref, q + 7)):
            moved = source[half:, :] if q == 0 else pltpu.roll(source[half:, :], 128 - 36 * q, 1)
            wide_ref[place] = jnp.where(keep, moved, 0.0)
    for q in range(4):
        wide_ref[q + 3] = jnp.concatenate([sup_ref[:, q, :].astype(f32), pad], axis=1)
    for q in range(10):
        at = 2 * HALO + 4 * q
        up_ref[at : at + 4, :] = wide_ref[q, blocks - 4 :, :]
        down_ref[at : at + 4, :] = wide_ref[q, :4, :]


def widen(perm, support, from_left, from_right):
    rows, blocks = perm.shape[0], support.shape[0]
    edge = jax.ShapeDtypeStruct((2 * HALO + 40, 128), f32)
    return pl.pallas_call(
        widen_kernel,
        out_shape=(
            jax.ShapeDtypeStruct((2, rows, 128), f32),
            jax.ShapeDtypeStruct((10, blocks, 128), f32),
            edge,
            edge,
        ),
        name="widen",
    )(perm, support, from_left, from_right)


def row_of(field, r):
    return field[pl.ds(r, 8, stride=PITCH), :]


def build_masks(field, sup, near, mask):
    for q in range(7):
        for i in range(SEG_BLOCKS + 4):
            for chunk in range(CHUNKS):
                near[q, i, 4 * chunk : 4 * chunk + 4, :] = sup[
                    pl.ds((q + 3 * chunk) * SUP_PITCH + i, 4, stride=SEG_BLOCKS), :
                ]
    lane = lanes()

    def region(step, carry):
        for tr in range(2):
            tile = 2 * step + tr
            r = jnp.clip(RIM + 16 * (tile - 2), RIM - 1, RIM + SEG_ROWS)
            inside = row_of(field, r) > 0.0
            for dx in SIDES:
                a = 2 * (1 - dx) + tr
                for ly in range(3):
                    column = window_lane(ly)
                    entry = column + 6 * a
                    chosen = jnp.take_along_axis(near[ly, step + dx + 1], entry, axis=1)
                    later = jnp.take_along_axis(near[ly + 3, step + dx + 1], entry, axis=1)
                    chosen = jnp.where(lane >= 16 + 32 * ly, later, chosen)
                    if ly == 0:
                        last = jnp.take_along_axis(near[6, step + dx + 1], entry, axis=1)
                        chosen = jnp.where(lane >= 112, last, chosen)
                    on = chosen == 1.0
                    if dx == 0:
                        on = on | ((column >= 2) & (column <= 3))
                    mask[tile, 3 * (dx + 1) + ly] = jnp.where(on & inside, f32(1.0), f32(0.0))
        return carry

    lax.fori_loop(0, SEG_BLOCKS + 2, region, 0)


def build_faces(field, coef, values):
    lane = lanes()
    starts = [(lane == 16) | (lane == 112), lane == 48, lane == 80]
    ends = [(lane == 15) | (lane == 111), lane == 47, lane == 79]
    own = [(window_lane(ly) >= 2) & (window_lane(ly) <= 3) for ly in range(3)]
    zero = jnp.zeros((8, 128), f32)

    def face(p, q):
        return 2.0 * p * q / jnp.maximum(p + q, TINY)

    def rows(step, carry):
        here, west = carry
        for u in range(6):
            r = FIRST + 6 * step + u
            there = row_of(field, r + 1)
            east = face(here, there)
            south = face(here, pltpu.roll(here, 1, 1))
            north = pltpu.roll(south, 127, 1)
            scale = 2.0 / jnp.maximum(west + east + south + north, TINY)
            coef[0, r] = scale * west
            coef[1, r] = scale * east
            south = scale * south
            north = scale * north
            for ly in range(3):
                coef[2 + ly, r] = jnp.where(starts[ly], 0.0, south)
                coef[5 + ly, r] = jnp.where(ends[ly], 0.0, north)
            for ly in range(3):
                values[0, 3 + ly, r] = jnp.where(own[ly] & (here > 0.0), f32(1.0), f32(0.0))
                values[0, ly, r] = zero
                values[0, 6 + ly, r] = zero
            here, west = there, east
        return here, west

    first = row_of(field, FIRST)
    lax.fori_loop(0, (LAST - FIRST) // 6, rows, (first, face(row_of(field, FIRST - 1), first)))
    for r in (FIRST - 1, LAST):
        inside = row_of(field, r) > 0.0
        for label in range(9):
            values[0, label, r] = zero
            values[1, label, r] = zero
        for ly in range(3):
            values[0, 3 + ly, r] = jnp.where(own[ly] & inside, f32(1.0), f32(0.0))


def smooth_row(values, coef, mask, now, r, tile, first_row, last_row):
    west, east = coef[0, r], coef[1, r]
    smoothed = []
    total = None
    for dx in SIDES:
        for ly in range(3):
            label = 3 * (dx + 1) + ly
            here = values[now, label, r]
            term = here
            if not first_row:
                term = term + west * values[now, label, r - 1]
            elif dx < 1:
                term = term + west * values[now, label + 3, r - 1]
            if not last_row:
                term = term + east * values[now, label, r + 1]
            elif dx > -1:
                term = term + east * values[now, label - 3, r + 1]
            term = term + coef[2 + ly, r] * pltpu.roll(here, 1, 1)
            term = term + coef[5 + ly, r] * pltpu.roll(here, 127, 1)
            term = mask[tile, label] * term
            smoothed.append(term)
            total = term if total is None else total + term
    inverse = 1.0 / jnp.maximum(total, TINY)
    for label in range(9):
        values[1 - now, label, r] = smoothed[label] * inverse


def iterate(values, coef, mask):
    def iteration(count, carry):
        now = lax.rem(count, 2)
        for r in range(FIRST, RIM):
            smooth_row(values, coef, mask, now, r, 1, False, r == RIM - 1)

        def region(b, inner):
            for u in range(32):
                smooth_row(
                    values, coef, mask, now, RIM + 32 * b + u, 2 * b + 2 + u // 16, u == 0, u == 31
                )
            return inner

        lax.fori_loop(0, SEG_BLOCKS, region, 0)
        for r in range(RIM + SEG_ROWS, LAST):
            smooth_row(values, coef, mask, now, r, 2 * SEG_BLOCKS + 2, r == RIM + SEG_ROWS, False)
        return carry

    lax.fori_loop(0, ITERS, iteration, 0)


def swap_groups(rows):
    group = lanes() // 16
    rows = list(rows)
    for bit in (1, 2, 4):
        upper = (group & bit) != 0
        for i in range(8):
            if i & bit == 0:
                a, b = rows[i], rows[i + bit]
                rows[i] = jnp.where(upper, pltpu.roll(b, 16 * bit, 1), a)
                rows[i + bit] = jnp.where(upper, b, pltpu.roll(a, 128 - 16 * bit, 1))
    return rows


def to_tiles(values, moved, b, dx, wraps):
    place = b + dx - 1 + (SEG_BLOCKS if wraps else 0)
    for tr in range(2):
        a = 2 * (1 - dx) + tr
        for half in range(2):
            r = RIM + 32 * b + 16 * tr + 8 * half
            for ly in range(3):
                groups = swap_groups([values[0, 3 * (dx + 1) + ly, r + u] for u in range(8)])
                for g in range(1, 7):
                    column = (g - 1 - 2 * ly) % 6
                    shift = 7 if wraps else 0
                    if (ly == 1 and g <= 2) or (ly == 2 and g >= 5):
                        shift = (shift + 4) % 8
                    tile = groups[g] if shift == 0 else pltpu.roll(groups[g], shift, 0)
                    at = 8 * (6 * a + column)
                    moved[ly, half, place, at : at + 8, :] = tile


def emit(moved, out, i, k):
    for q, (array, at) in enumerate(((0, 0), (1, 0), (2, 4), (0, 4))):
        for half in range(2):
            for t in range(0, 36, 8):
                count = min(8, 36 - t)
                out[i + SEG_BLOCKS * k, q, t : t + count, 128 * half : 128 * half + 128] = moved[
                    array, half, i, pl.ds(8 * t + at + k, count, stride=8), :
                ]


def main_kernel(
    field_hbm, sup_ref, low_ref, high_ref, out, field, sup, near, mask, coef, values, moved, sem
):
    rows = field_hbm.shape[1]
    blocks = sup_ref.shape[1]
    copies = []
    for chunk in range(CHUNKS):
        for k in range(SEGMENTS):
            start = SEG_ROWS * k - HALO
            begin, end = max(start, 0), min(start + PITCH, rows)
            base = (4 * chunk + k) * PITCH
            copy = pltpu.make_async_copy(
                field_hbm.at[chunk, pl.ds(begin, end - begin), :],
                field.at[pl.ds(base + begin - start, end - begin), :],
                sem.at[4 * chunk + k],
            )
            copy.start()
            copies.append(copy)
    for q in range(10):
        at = q * SUP_PITCH
        sup[at : at + 3, :] = low_ref[2 * HALO + 4 * q + 1 : 2 * HALO + 4 * q + 4, :]
        sup[at + 3 : at + 3 + blocks, :] = sup_ref[q]
        sup[at + 3 + blocks : at + 6 + blocks, :] = high_ref[2 * HALO + 4 * q : 2 * HALO + 4 * q + 3, :]
        sup[at + 6 + blocks : at + SUP_PITCH, :] = jnp.zeros((SUP_PITCH - 6 - blocks, 128), f32)
    for copy in copies:
        copy.wait()
    for chunk in range(CHUNKS):
        base = 4 * chunk * PITCH
        field[base : base + HALO, :] = low_ref[chunk * HALO : (chunk + 1) * HALO, :]
        base = base + 3 * PITCH
        top = rows - (3 * SEG_ROWS - HALO)
        field[base + top : base + top + HALO, :] = high_ref[chunk * HALO : (chunk + 1) * HALO, :]
        field[base + top + HALO : base + PITCH, :] = jnp.zeros((PITCH - HALO - top, 128), f32)
    build_masks(field, sup, near, mask)
    build_faces(field, coef, values)
    iterate(values, coef, mask)
    for dx in SIDES:
        to_tiles(values, moved, 0, dx, dx < 1)
    for dx in SIDES:
        to_tiles(values, moved, 1, dx, dx < 0)

    def region(b, carry):
        for dx in SIDES:
            to_tiles(values, moved, b, dx, False)
        return carry

    lax.fori_loop(2, SEG_BLOCKS, region, 0)

    def block(i, carry):
        for k in range(3):
            emit(moved, out, i, k)
        return carry

    lax.fori_loop(0, SEG_BLOCKS, block, 0)

    def last_block(i, carry):
        emit(moved, out, i, 3)
        return carry

    lax.fori_loop(0, blocks - 3 * SEG_BLOCKS, last_block, 0)


def smooth(field, sup, low, high):
    blocks = sup.shape[1]
    vmem = pl.BlockSpec(memory_space=pltpu.VMEM)
    return pl.pallas_call(
        main_kernel,
        out_shape=jax.ShapeDtypeStruct((blocks, 4, 36, 256), f32),
        in_specs=[pl.BlockSpec(memory_space=pl.ANY), vmem, vmem, vmem],
        out_specs=vmem,
        scratch_shapes=[
            pltpu.VMEM((8 * PITCH, 128), f32),
            pltpu.VMEM((10 * SUP_PITCH, 128), f32),
            pltpu.VMEM((7, SEG_BLOCKS + 4, 8, 128), f32),
            pltpu.VMEM((2 * SEG_BLOCKS + 4, 9, 8, 128), f32),
            pltpu.VMEM((8, PITCH, 8, 128), f32),
            pltpu.VMEM((2, 9, PITCH, 8, 128), f32),
            pltpu.VMEM((3, 2, SEG_BLOCKS, 36 * 8, 128), f32),
            pltpu.SemaphoreType.DMA((8,)),
        ],
        compiler_params=pltpu.CompilerParams(vmem_limit_bytes=60 * 1024 * 1024),
        name="smooth",
    )(field, sup, low, high)


def neighbours(up, down, axis):
    count = lax.axis_size(axis)
    forward = [(i, i + 1) for i in range(count - 1)]
    backward = [(i + 1, i) for i in range(count - 1)]
    return lax.ppermute(up, axis, forward), lax.ppermute(down, axis, backward)


def body(permeability, support):
    up, down = pack(permeability, support)
    from_left, from_right = neighbours(up, down, "gy")
    field, sup, up, down = widen(permeability, support, from_left, from_right)
    low, high = neighbours(up, down, "gx")
    return smooth(field, sup, low, high)


def solution(mesh):
    return jax.shard_map(
        body,
        mesh=mesh,
        in_specs=(P(("grp", "gx"), "gy"), P(("grp", "gx"), "gy", None)),
        out_specs=P(("grp", "gx"), "gy", None, None),
        check_vma=False,
    )
```

time: 575 us -> 213 us (0.37)
  local copies, waits for them, and re-layouts: 279 us -> 7.86 us
  Pallas kernels: 0 us -> 181 us
  other arithmetic: 153 us -> 0 us
  starting transfers between devices: 79.7 us -> 12.1 us
  waiting for transfers between devices: 57.9 us -> 11.8 us
    pallas_call x0 -> x3, Pallas kernels: none -> 181 us  [the longest x1 176 us: smooth(): pl.pallas_call(main_kernel, out_shape=jax.ShapeDtypeStruct((blocks, 4, 36...]
    reshape x3 -> x0, local copies, waits for them, and re-layouts: 116 us -> none  [the longest x1 55.2 us: pieces_to_tiles(): values.reshape(3, 3, blocks_x, 2, 16, blocks_y, 2, 16)]
    select_n x9 -> x0, other arithmetic: 98.3 us -> none  [the longest x4 88.4 us: smooth_pieces(): jnp.where(cell_mask, (1.0 - OMEGA) * values + OMEGA * beside / diag, jnp....]
    ppermute x36 -> x4, starting transfers between devices: 79.7 us -> 12.1 us  [neighbours(): return (lax.ppermute(up, axis, forward), lax.ppermute(down, axis, backward))]
    while x41 -> x0, local copies, waits for them, and re-layouts: 61.5 us -> none  [the longest x9 46.8 us: body(): final = lax.fori_loop(0, ITERS, iterate, start)]
    transpose x1 -> x0, local copies, waits for them, and re-layouts: 48.4 us -> none  [pieces_to_tiles(): values.reshape(3, 3, blocks_x, 2, 16, blocks_y, 2, 16)]
    ppermute x36 -> x4, waiting for transfers between devices: 57.9 us -> 11.8 us  [neighbours(): return (lax.ppermute(up, axis, forward), lax.ppermute(down, axis, backward))]
    another operation x41 -> x0, other arithmetic: 32.6 us -> none  [the longest x28 25.3 us: by_offset(): jnp.stack([jnp.stack([field[32 * r:32 * r + rows, 32 * c:32 * c + cols] f...]
  transfers between devices with their start and end apart: 36 -> 4, of which waited for: 20 -> 3; matrix products, arithmetic and copies ran while one was open for 17% -> 0% of each run, Pallas kernels for 0% -> 0%
where the time goes in v1:
time: 213 us
  Pallas kernels  181 us (85%)
  starting transfers between devices  12.1 us (6%)
  waiting for transfers between devices  11.8 us (6%)
  local copies, waits for them, and re-layouts  7.86 us (4%)
    pallas_call x1, Pallas kernels, smooth(): pl.pallas_call(main_kernel, out_shape=jax.ShapeDtypeStruct((blocks, 4, 36...  176 us
    ppermute x4, starting transfers between devices, neighbours(): return (lax.ppermute(up, axis, forward), lax.ppermute(down, axis, backward))  12.1 us
    ppermute x4, waiting for transfers between devices, neighbours(): return (lax.ppermute(up, axis, forward), lax.ppermute(down, axis, backward))  11.8 us
    pallas_call x1, local copies, waits for them, and re-layouts, smooth(): pl.pallas_call(main_kernel, out_shape=jax.ShapeDtypeStruct((blocks, 4, 36...  6.54 us
  transfers between devices with their start and end apart: 4, of which 3 were waited for; matrix products, arithmetic and copies ran while one was open for 0% of the time, Pallas kernels for 0%

profile of v1, /device:TPU:1, one launch (start us, length us, event | category | flops | bytes accessed | tf_op | source)
XLA Modules:
  0.0 212.9 jit_solution(2930085512342621764)
XLA Ops:
  0.0 2.0 pack.1
  2.0 4.0 %collective-permute-start = (f32[544,128]{1,0:T(8,128)}, f32[544,128]{1,0:T(8,128)S(1)}, u32[]{:S(2)}, u32[]{:S(2)}) collective-permute-start(f32[544,128]{1,0:T(8,128)} %get-tuple-element.11), channel_id=1, source_target_pairs={{0,1},{1,2},{2,3},{4,5},{5,6},{6,7},{8,9},{9,10},{10,11},{12,13},{... | collective-permute-start | bytes 835592 | tf_op jit(solution)/shard_map/ppermute | solution.py:364
  6.1 1.3 collective-permute-start.1
  7.4 4.3 %collective-permute-done.left_ref = f32[544,128]{1,0:T(8,128)S(1)} collective-permute-done((f32[544,128]{1,0:T(8,128)}, f32[544,128]{1,0:T(8,128)S(1)}, u32[]{:S(2)}, u32[]{:S(2)}) %collective-permute-start) | collective-permute-done | bytes 278560 | tf_op jit(solution)/shard_map/ppermute | solution.py:364
  11.7 0.0 copy-start
  11.7 3.7 %collective-permute-done.1.right_ref = f32[544,128]{1,0:T(8,128)S(1)} collective-permute-done((f32[544,128]{1,0:T(8,128)}, f32[544,128]{1,0:T(8,128)S(1)}, u32[]{:S(2)}, u32[]{:S(2)}) %collective-permute-start.1) | collective-permute-done | bytes 278560 | tf_op jit(solution)/shard_map/ppermute | solution.py:364
  15.4 0.0 copy-done
  15.4 0.0 copy-start.1
  15.4 0.7 copy-done.1
  16.1 2.9 %widen.1 = (f32[2,1024,128]{2,1,0:T(8,128)}, f32[10,32,128]{2,1,0:T(8,128)}, f32[120,128]{1,0:T(8,128)}, f32[120,128]{1,0:T(8,128)}) custom-call(f32[1024,128]{1,0:T(8,128)} %perm_ref.3, s32[32,4,36]{2,1,0:T(4,128)} %sup_ref.3, f32[544,128]{1,0:T(8,128)} %copy-done, f32[544,128]{1,0:T(8,128)} %copy-done.1), custom_call_target="tpu_custom_call" | custom-call | tf_op jit(solution)/shard_map/widen/pallas_call | solution.py:92
  19.0 4.9 %collective-permute-start.2 = (f32[120,128]{1,0:T(8,128)}, f32[120,128]{1,0:T(8,128)S(1)}, u32[]{:S(2)}, u32[]{:S(2)}) collective-permute-start(f32[120,128]{1,0:T(8,128)} %get-tuple-element.15), channel_id=1, source_target_pairs={{0,4},{4,8},{8,12},{1,5},{5,9},{9,13},{2,6},{6,10},{10,14},{3,7},{... | collective-permute-start | bytes 184328 | tf_op jit(solution)/shard_map/ppermute | solution.py:364
  23.9 1.9 collective-permute-start.3
  25.8 0.0 collective-permute-done.2.low_ref
  25.8 0.0 copy-start.2
  25.8 3.8 %collective-permute-done.3.high_ref = f32[120,128]{1,0:T(8,128)S(1)} collective-permute-done((f32[120,128]{1,0:T(8,128)}, f32[120,128]{1,0:T(8,128)S(1)}, u32[]{:S(2)}, u32[]{:S(2)}) %collective-permute-start.3) | collective-permute-done | bytes 61472 | tf_op jit(solution)/shard_map/ppermute | solution.py:364
  29.6 0.0 copy-start.3
  29.6 0.0 copy-done.2
  29.6 0.6 copy-done.3
  30.2 176.1 %smooth.1 = f32[32,4,36,256]{3,2,1,0:T(8,128)} custom-call(f32[2,1024,128]{2,1,0:T(8,128)} %get-tuple-element.13.field_hbm, f32[10,32,128]{2,1,0:T(8,128)} %get-tuple-element.14.sup_ref, f32[120,128]{1,0:T(8,128)} %copy-done.2, f32[120,128]{1,0:T(8,128)} %copy-done.3), custom_call_target="tpu_custom_call" | custom-call | tf_op jit(solution)/shard_map/smooth/pallas_call | solution.py:340
  206.3 6.5 %copy.3 = f32[32,4,36,256]{3,1,2,0:T(4,128)} copy(f32[32,4,36,256]{3,2,1,0:T(8,128)} %smooth.1) | data formatting | bytes 9437184 | tf_op jit(solution)/shard_map/smooth/pallas_call | solution.py:340
Async XLA Ops:
  2.0 9.6 %collective-permute-start = (f32[544,128]{1,0:T(8,128)}, f32[544,128]{1,0:T(8,128)S(1)}, u32[]{:S(2)}, u32[]{:S(2)}) collective-permute-start(f32[544,128]{1,0:T(8,128)} %get-tuple-element.11), channel_id=1, source_target_pairs={{0,1},{1,2},{2,3},{4,5},{5,6},{6,7},{8,9},{9,10},{10,11},{12,13},{... | collective-permute-start | bytes 835592 | tf_op jit(solution)/shard_map/ppermute | solution.py:364
  6.1 9.3 %collective-permute-start.1 = (f32[544,128]{1,0:T(8,128)}, f32[544,128]{1,0:T(8,128)S(1)}, u32[]{:S(2)}, u32[]{:S(2)}) collective-permute-start(f32[544,128]{1,0:T(8,128)} %get-tuple-element.12), channel_id=1, source_target_pairs={{1,0},{2,1},{3,2},{5,4},{6,5},{7,6},{9,8},{10,9},{11,10},{13,12},{... | collective-permute-start | bytes 835592 | tf_op jit(solution)/shard_map/ppermute | solution.py:364
  11.7 3.7 %copy-start = (f32[544,128]{1,0:T(8,128)}, f32[544,128]{1,0:T(8,128)S(1)}, u32[]{:S(2)}) copy-start(f32[544,128]{1,0:T(8,128)S(1)} %collective-permute-done.left_ref) | copy-start | bytes 835588
  15.4 0.7 copy-start.1
  19.0 6.8 %collective-permute-start.2 = (f32[120,128]{1,0:T(8,128)}, f32[120,128]{1,0:T(8,128)S(1)}, u32[]{:S(2)}, u32[]{:S(2)}) collective-permute-start(f32[120,128]{1,0:T(8,128)} %get-tuple-element.15), channel_id=1, source_target_pairs={{0,4},{4,8},{8,12},{1,5},{5,9},{9,13},{2,6},{6,10},{10,14},{3,7},{... | collective-permute-start | bytes 184328 | tf_op jit(solution)/shard_map/ppermute | solution.py:364
  23.9 5.8 %collective-permute-start.3 = (f32[120,128]{1,0:T(8,128)}, f32[120,128]{1,0:T(8,128)S(1)}, u32[]{:S(2)}, u32[]{:S(2)}) collective-permute-start(f32[120,128]{1,0:T(8,128)} %get-tuple-element.16), channel_id=1, source_target_pairs={{4,0},{8,4},{12,8},{5,1},{9,5},{13,9},{6,2},{10,6},{14,10},{7,3},{... | collective-permute-start | bytes 184328 | tf_op jit(solution)/shard_map/ppermute | solution.py:364
  25.8 3.8 %copy-start.2 = (f32[120,128]{1,0:T(8,128)}, f32[120,128]{1,0:T(8,128)S(1)}, u32[]{:S(2)}) copy-start(f32[120,128]{1,0:T(8,128)S(1)} %collective-permute-done.2.low_ref) | copy-start | bytes 184324
  29.6 0.6 copy-start.3

commit v2 on v0

v2 whole, which is shorter than its diff:
```python
import jax
import jax.numpy as jnp
from jax import lax
from jax.experimental import pallas as pl
from jax.experimental.pallas import tpu as pltpu
from jax.sharding import PartitionSpec as P

ITERS = 4
SIDES = (-1, 0, 1)
TINY = 1e-30
OFF = 2.0

RIM = 4
PAD = 8
HIGH = 32 + 2 * RIM
PITCH = 64 + 2 * PAD
BANDS = 3
LANE_PITCH = 40
HALO = 40
WIDTH = 32 + RIM
FIELD_ROWS = 32 * LANE_PITCH + 16
SUP_PITCH = 48
BLOCK_ROWS = 36 * 8

f32 = jnp.float32


def groups_of(rows):
    third = -(-rows // 24) * 8
    return [(g, g * third, min(third, rows - g * third)) for g in range(3)]


def pack_kernel(perm_ref, sup_ref, up_ref, down_ref):
    rows = perm_ref.shape[0]
    parts = groups_of(rows)
    third = parts[0][2]
    lane = lax.broadcasted_iota(jnp.int32, (third, 128), 1)
    up = down = None
    for g, start, count in parts:
        part = perm_ref[start : start + count, :]
        if count < third:
            part = jnp.concatenate([part, jnp.zeros((third - count, 128), f32)], axis=0)
        high = pltpu.roll(part, WIDTH * (g + 1), 1)
        low = part if g == 0 else pltpu.roll(part, WIDTH * g, 1)
        up = high if up is None else jnp.where(lane < WIDTH * g, up, high)
        down = low if down is None else jnp.where(lane < WIDTH * g, down, low)
    up_ref[:third, :] = up
    down_ref[:third, :] = down
    blocks = sup_ref.shape[0]
    pad = jnp.zeros((blocks, 92), f32)
    wide = [
        jnp.concatenate([sup_ref[:, q, :].astype(f32), pad], axis=1) for q in range(4)
    ]
    up_ref[third:, :] = wide[1] + pltpu.roll(wide[2], 36, 1) + pltpu.roll(wide[3], 72, 1)
    down_ref[third:, :] = wide[0] + pltpu.roll(wide[1], 36, 1) + pltpu.roll(wide[2], 72, 1)


def pack(perm, support):
    third = groups_of(perm.shape[0])[0][2]
    shape = jax.ShapeDtypeStruct((third + support.shape[0], 128), f32)
    return pl.pallas_call(pack_kernel, out_shape=(shape, shape), name="pack")(perm, support)


def widen_kernel(perm_ref, sup_ref, left_ref, right_ref, field_ref, wide_ref, up_ref, down_ref):
    rows = perm_ref.shape[0]
    for g, start, count in groups_of(rows):
        lane = lax.broadcasted_iota(jnp.int32, (count, 128), 1)
        own = perm_ref[start : start + count, :]
        moved = pltpu.roll(own, WIDTH, 1)
        left, right = left_ref[:count, :], right_ref[:count, :]
        if g > 0:
            left = pltpu.roll(left, 128 - WIDTH * g, 1)
        if g != 1:
            right = pltpu.roll(right, (128 + WIDTH - WIDTH * g) % 128, 1)
        field_ref[0, start : start + count, :] = jnp.where(lane < WIDTH, left, moved)
        field_ref[1, start : start + count, :] = pltpu.roll(own, 128 - (64 - WIDTH), 1)
        field_ref[2, start : start + count, :] = jnp.where(
            lane < WIDTH, moved, jnp.where(lane < 2 * WIDTH, right, 0.0)
        )
    for place, band in enumerate((0, 2)):
        up_ref[place * HALO : (place + 1) * HALO, :] = field_ref[band, rows - HALO :, :]
        down_ref[place * HALO : (place + 1) * HALO, :] = field_ref[band, :HALO, :]
    blocks = sup_ref.shape[0]
    third = groups_of(rows)[0][2]
    keep = lax.broadcasted_iota(jnp.int32, (blocks, 128), 1) < 36
    pad = jnp.zeros((blocks, 92), f32)
    for q in range(3):
        for source, place in ((left_ref, q), (right_ref, q + 7)):
            moved = source[third:, :] if q == 0 else pltpu.roll(source[third:, :], 128 - 36 * q, 1)
            wide_ref[place] = jnp.where(keep, moved, 0.0)
    for q in range(4):
        wide_ref[q + 3] = jnp.concatenate([sup_ref[:, q, :].astype(f32), pad], axis=1)
    for q in range(10):
        at = 2 * HALO + 4 * q
        up_ref[at : at + 4, :] = wide_ref[q, blocks - 4 :, :]
        down_ref[at : at + 4, :] = wide_ref[q, :4, :]


def widen(perm, support, from_left, from_right):
    rows, blocks = perm.shape[0], support.shape[0]
    edge = jax.ShapeDtypeStruct((2 * HALO + 40, 128), f32)
    return pl.pallas_call(
        widen_kernel,
        out_shape=(
            jax.ShapeDtypeStruct((BANDS, rows, 128), f32),
            jax.ShapeDtypeStruct((10, blocks, 128), f32),
            edge,
            edge,
        ),
        name="widen",
    )(perm, support, from_left, from_right)


def build_cells(field, cells):
    blank = jnp.zeros((128 - BANDS * LANE_PITCH, 128), f32)
    edge = jnp.zeros((PAD - RIM, 128), f32)

    def row(x, carry):
        parts = [
            field[pl.ds(band * FIELD_ROWS + 256 * m + x + HALO - WIDTH, 8, stride=32), :]
            for band in range(BANDS)
            for m in range(LANE_PITCH // 8)
        ]
        turned = jnp.concatenate(parts + [blank], axis=0).T
        cells[x, 0 : PAD - RIM, :] = edge
        cells[x, PAD - RIM : PITCH - PAD + RIM, :] = turned[: 64 + 2 * RIM]
        cells[x, PITCH - PAD + RIM : PITCH, :] = edge
        return carry

    lax.fori_loop(0, HIGH, row, 0)


PIECES = (
    (PAD - RIM, RIM, 0, 1),
    (PAD, 16, 1, 0),
    (PAD + 16, 16, 1, 1),
    (PAD + 32, 16, 2, 0),
    (PAD + 48, 16, 2, 1),
    (PAD + 64, RIM, 3, 0),
)


def side_of(label, region):
    return (label - region + 1) % 3 - 1


def build_masks(cells, sup, turned, mask):
    blank = jnp.zeros((128 - BANDS * LANE_PITCH, 128), f32)
    for ex in range(5):
        for ey in range(6):
            parts = [
                sup[(2 * band + ey) * SUP_PITCH + ex : (2 * band + ey) * SUP_PITCH + ex + LANE_PITCH, :]
                for band in range(BANDS)
            ]
            turned[ex, ey] = jnp.concatenate(parts + [blank], axis=0).T[:40]
    for tile, (x, rx, tr) in enumerate(
        ((RIM - 1, 0, 1), (RIM, 1, 0), (RIM + 16, 1, 1), (RIM + 32, 2, 0))
    ):
        for start, count, region, tc in PIECES:
            inside = cells[x, start : start + 1, :] > 0.0
            for dx in SIDES:
                for label in range(3):
                    dy = side_of(label, region)
                    if dx == 0 and dy == 0:
                        on = inside
                    else:
                        t = 6 * (2 * (1 - dx) + tr) + 2 * (1 - dy) + tc
                        on = inside & (turned[rx + dx + 1, region + dy + 1, t : t + 1, :] == 1.0)
                    mask[tile, 3 * (dx + 1) + label, start : start + count, :] = jnp.broadcast_to(
                        jnp.where(on, f32(1.0), f32(0.0)), (count, 128)
                    )


def build_faces(cells, coef, values):
    starts = [PAD - RIM + 8 * m for m in range(9)]
    zero = jnp.zeros((8, 128), f32)
    sub = lax.broadcasted_iota(jnp.int32, (8, 128), 0)

    def face(p, q):
        return 2.0 * p * q / jnp.maximum(p + q, TINY)

    def row(x, west):
        east, south = [], []
        for z in starts:
            here = cells[x, z : z + 8, :]
            east.append(face(here, cells[x + 1, z : z + 8, :]))
            south.append(face(here, cells[x, z - 1 : z + 7, :]))
        for m, z in enumerate(starts):
            after = south[m + 1] if m < 8 else zero
            north = jnp.where(sub == 7, pltpu.roll(after, 7, 0), pltpu.roll(south[m], 7, 0))
            scale = OFF / jnp.maximum(west[m] + east[m] + south[m] + north, TINY)
            coef[0, x, z : z + 8, :] = scale * west[m]
            coef[1, x, z : z + 8, :] = scale * east[m]
            coef[2, x, z : z + 8, :] = scale * south[m]
            coef[3, x, z : z + 8, :] = scale * north
        return tuple(east)

    first = tuple(face(cells[0, z : z + 8, :], cells[1, z : z + 8, :]) for z in starts)
    lax.fori_loop(1, HIGH - 1, row, first)

    def begin(x, carry):
        for dx in SIDES:
            for label in range(3):
                for start, count, region, tc in PIECES:
                    own = dx == 0 and side_of(label, region) == 0
                    inside = cells[x, start : start + count, :] > 0.0
                    values[3 * (dx + 1) + label, x, start : start + count, :] = (
                        jnp.where(inside, f32(1.0), f32(0.0)) if own else jnp.zeros((count, 128), f32)
                    )
        return carry

    lax.fori_loop(0, HIGH, begin, 0)


def cut(field, z, edge):
    if not z <= edge < z + 8:
        return field
    sub = lax.broadcasted_iota(jnp.int32, (8, 128), 0)
    return jnp.where(sub == edge - z, 0.0, field)


def smooth_row(old, new, coef, mask, x, tile, starts, first_row, last_row):
    for z in starts:
        rows = slice(z, z + 8)
        west, east = coef[0, x, rows, :], coef[1, x, rows, :]
        south, north = coef[2, x, rows, :], coef[3, x, rows, :]
        edges = (PAD + 32, PAD + 64, PAD)
        souths = [cut(south, z, edge) for edge in edges]
        norths = [cut(north, z, edge - 1) for edge in edges]
        smoothed = []
        total = None
        for dx in SIDES:
            for label in range(3):
                at = 3 * (dx + 1) + label
                term = old[at, x, rows, :]
                if not first_row:
                    term = term + west * old[at, x - 1, rows, :]
                elif dx < 1:
                    term = term + west * old[at + 3, x - 1, rows, :]
                if not last_row:
                    term = term + east * old[at, x + 1, rows, :]
                elif dx > -1:
                    term = term + east * old[at - 3, x + 1, rows, :]
                term = term + souths[label] * old[at, x, z - 1 : z + 7, :]
                term = term + norths[label] * old[at, x, z + 1 : z + 9, :]
                term = mask[tile, at, rows, :] * term
                smoothed.append(term)
                total = term if total is None else total + term
        inverse = 1.0 / jnp.maximum(total, TINY)
        for at in range(9):
            new[at, x, rows, :] = smoothed[at] * inverse


def iterate(old, new, coef, mask, rim):
    if rim:
        starts = [PAD - RIM + 8 * m for m in range(9)]
    else:
        starts = [PAD + 8 * m for m in range(8)]

    def rows(begin, end, tile, first_row=False, last_row=False):
        if end - begin > 1:

            def step(x, carry):
                smooth_row(old, new, coef, mask, x, tile, starts, False, False)
                return carry

            lax.fori_loop(begin, end, step, 0)
        elif end > begin:
            smooth_row(old, new, coef, mask, begin, tile, starts, first_row, last_row)

    rows(RIM - rim, RIM - 1, 0)
    if rim:
        rows(RIM - 1, RIM, 0, last_row=True)
    rows(RIM, RIM + 1, 1, first_row=True)

    def inner(x, carry):
        tile = jnp.where(x < RIM + 16, 1, 2)
        smooth_row(old, new, coef, mask, x, tile, starts, False, False)
        return carry

    lax.fori_loop(RIM + 1, RIM + 31, inner, 0)
    rows(RIM + 31, RIM + 32, 2, last_row=True)
    if rim:
        rows(RIM + 32, RIM + 33, 3, first_row=True)
    rows(RIM + 33, RIM + 32 + rim, 3)


def to_tiles(values, out):
    def half_tile(part, carry):
        for dx in SIDES:
            for label in range(3):
                for tc in range(4):
                    z = PAD + 16 * tc
                    region = 1 + tc // 2
                    dy = side_of(label, region)
                    cells = [
                        values[3 * (dx + 1) + label, RIM + 8 * part + u, z : z + 16, :]
                        for u in range(8)
                    ]
                    turned = jnp.concatenate(cells, axis=0).T
                    t = 12 * (1 - dx) + 2 * (1 - dy) + tc % 2
                    for band in range(BANDS):
                        q = 2 * band - 2 + region + dy
                        if 0 <= q < 4:
                            for m in range(LANE_PITCH // 8):
                                row = (8 * m + 1 + dx) * BLOCK_ROWS + 8 * t + q
                                out[
                                    pl.ds(row + (part // 2) * 48 + (part % 2) * 4, 8, stride=BLOCK_ROWS), :
                                ] = turned[LANE_PITCH * band + 8 * m : LANE_PITCH * band + 8 * m + 8]
        return carry

    lax.fori_loop(0, 4, half_tile, 0)


def main_kernel(
    field_hbm, sup_ref, low_ref, high_ref, out_hbm,
    field, sup, cells, turned, mask, coef, values, other, out, sem,
):
    rows = field_hbm.shape[1]
    blocks = sup_ref.shape[1]
    copies = []
    for band in range(BANDS):
        copy = pltpu.make_async_copy(
            field_hbm.at[band],
            field.at[pl.ds(band * FIELD_ROWS + HALO, rows), :],
            sem.at[band],
        )
        copy.start()
        copies.append(copy)
    lane = lax.broadcasted_iota(jnp.int32, (HALO, 128), 1)
    for ref, at in ((low_ref, 0), (high_ref, HALO + rows)):
        left, right = ref[:HALO, :], ref[HALO : 2 * HALO, :]
        field[at : at + HALO, :] = left
        at = at + FIELD_ROWS
        field[at : at + HALO, :] = jnp.where(lane < 64, pltpu.roll(left, 64, 1), pltpu.roll(right, 64, 1))
        at = at + FIELD_ROWS
        field[at : at + HALO, :] = right
    rest = FIELD_ROWS - rows - 2 * HALO
    for band in range(BANDS):
        at = band * FIELD_ROWS + rows + 2 * HALO
        field[at : at + rest, :] = jnp.zeros((rest, 128), f32)
    for q in range(10):
        at = q * SUP_PITCH
        sup[at : at + 3, :] = low_ref[2 * HALO + 4 * q + 1 : 2 * HALO + 4 * q + 4, :]
        sup[at + 3 : at + 3 + blocks, :] = sup_ref[q]
        sup[at + 3 + blocks : at + 6 + blocks, :] = high_ref[2 * HALO + 4 * q : 2 * HALO + 4 * q + 3, :]
        sup[at + 6 + blocks : at + SUP_PITCH, :] = jnp.zeros((SUP_PITCH - 6 - blocks, 128), f32)
    for copy in copies:
        copy.wait()
    build_cells(field, cells)
    build_masks(cells, sup, turned, mask)
    build_faces(cells, coef, values)
    for count in range(ITERS):
        old, new = (values, other) if count % 2 == 0 else (other, values)
        iterate(old, new, coef, mask, ITERS - 1 - count)
    to_tiles(values if ITERS % 2 == 0 else other, out)
    copy = pltpu.make_async_copy(
        out.at[pl.ds(2 * BLOCK_ROWS, blocks * BLOCK_ROWS), :], out_hbm, sem.at[0]
    )
    copy.start()
    copy.wait()


def smooth(field, sup, low, high):
    blocks = sup.shape[1]
    vmem = pl.BlockSpec(memory_space=pltpu.VMEM)
    hbm = pl.BlockSpec(memory_space=pl.ANY)
    return pl.pallas_call(
        main_kernel,
        out_shape=jax.ShapeDtypeStruct((blocks * BLOCK_ROWS, 128), f32),
        in_specs=[hbm, vmem, vmem, vmem],
        out_specs=hbm,
        scratch_shapes=[
            pltpu.VMEM((BANDS * FIELD_ROWS, 128), f32),
            pltpu.VMEM((10 * SUP_PITCH, 128), f32),
            pltpu.VMEM((HIGH, PITCH, 128), f32),
            pltpu.VMEM((5, 6, 40, 128), f32),
            pltpu.VMEM((4, 9, PITCH, 128), f32),
            pltpu.VMEM((4, HIGH, PITCH, 128), f32),
            pltpu.VMEM((9, HIGH, PITCH, 128), f32),
            pltpu.VMEM((9, HIGH, PITCH, 128), f32),
            pltpu.VMEM(((LANE_PITCH + 2) * BLOCK_ROWS, 128), f32),
            pltpu.SemaphoreType.DMA((BANDS,)),
        ],
        compiler_params=pltpu.CompilerParams(vmem_limit_bytes=60 * 1024 * 1024),
        name="smooth",
    )(field, sup, low, high)


def neighbours(up, down, axis):
    count = lax.axis_size(axis)
    forward = [(i, i + 1) for i in range(count - 1)]
    backward = [(i + 1, i) for i in range(count - 1)]
    return lax.ppermute(up, axis, forward), lax.ppermute(down, axis, backward)


def body(permeability, support):
    up, down = pack(permeability, support)
    from_left, from_right = neighbours(up, down, "gy")
    field, sup, up, down = widen(permeability, support, from_left, from_right)
    low, high = neighbours(up, down, "gx")
    tiles = smooth(field, sup, low, high).reshape(support.shape[0], 36, 2, 4, 128)
    return tiles.transpose(0, 3, 1, 2, 4).reshape(support.shape + (256,))


def solution(mesh):
    return jax.shard_map(
        body,
        mesh=mesh,
        in_specs=(P(("grp", "gx"), "gy"), P(("grp", "gx"), "gy", None)),
        out_specs=P(("grp", "gx"), "gy", None, None),
        check_vma=False,
    )
```

time: 575 us -> 70.3 us (0.12)
  local copies, waits for them, and re-layouts: 279 us -> 1.3 us
  other arithmetic: 153 us -> 0 us
  starting transfers between devices: 79.7 us -> 12.1 us
  waiting for transfers between devices: 57.9 us -> 9.97 us
  Pallas kernels: 0 us -> 46.6 us
    reshape x3 -> x0, local copies, waits for them, and re-layouts: 116 us -> none  [the longest x1 55.2 us: pieces_to_tiles(): values.reshape(3, 3, blocks_x, 2, 16, blocks_y, 2, 16)]
    select_n x9 -> x0, other arithmetic: 98.3 us -> none  [the longest x4 88.4 us: smooth_pieces(): jnp.where(cell_mask, (1.0 - OMEGA) * values + OMEGA * beside / diag, jnp....]
    ppermute x36 -> x4, starting transfers between devices: 79.7 us -> 12.1 us  [neighbours(): return (lax.ppermute(up, axis, forward), lax.ppermute(down, axis, backward))]
    while x41 -> x0, local copies, waits for them, and re-layouts: 61.5 us -> none  [the longest x9 46.8 us: body(): final = lax.fori_loop(0, ITERS, iterate, start)]
    transpose x1 -> x0, local copies, waits for them, and re-layouts: 48.4 us -> none  [pieces_to_tiles(): values.reshape(3, 3, blocks_x, 2, 16, blocks_y, 2, 16)]
    ppermute x36 -> x4, waiting for transfers between devices: 57.9 us -> 9.97 us  [neighbours(): return (lax.ppermute(up, axis, forward), lax.ppermute(down, axis, backward))]
    pallas_call x0 -> x3, Pallas kernels: none -> 46.6 us  [the longest x1 41.6 us: smooth(): pl.pallas_call(main_kernel, out_shape=jax.ShapeDtypeStruct((blocks * BLOC...]
    another operation x41 -> x0, other arithmetic: 32.6 us -> none  [the longest x28 25.3 us: by_offset(): jnp.stack([jnp.stack([field[32 * r:32 * r + rows, 32 * c:32 * c + cols] f...]
  transfers between devices with their start and end apart: 36 -> 4, of which waited for: 20 -> 3; matrix products, arithmetic and copies ran while one was open for 17% -> 0% of each run, Pallas kernels for 0% -> 0%
where the time goes in v2:
time: 70.3 us; the launch traced here: 70 us
  Pallas kernels  46.6 us (66%)
  starting transfers between devices  12.1 us (17%)
  waiting for transfers between devices  9.97 us (14%)
  local copies, waits for them, and re-layouts  1.3 us (2%)
    pallas_call x1, Pallas kernels, smooth(): pl.pallas_call(main_kernel, out_shape=jax.ShapeDtypeStruct((blocks * BLOC...  41.6 us
    ppermute x4, starting transfers between devices, neighbours(): return (lax.ppermute(up, axis, forward), lax.ppermute(down, axis, backward))  12.1 us
    ppermute x4, waiting for transfers between devices, neighbours(): return (lax.ppermute(up, axis, forward), lax.ppermute(down, axis, backward))  9.97 us
    pallas_call x1, Pallas kernels, widen(): pl.pallas_call(widen_kernel, out_shape=(jax.ShapeDtypeStruct((BANDS, rows...  2.95 us
    pallas_call x1, Pallas kernels, pack(): pl.pallas_call(pack_kernel, out_shape=(shape, shape), name='pack')  2.07 us
  transfers between devices with their start and end apart: 4, of which 3 were waited for; matrix products, arithmetic and copies ran while one was open for 0% of the time, Pallas kernels for 0%

profile of v2, /device:TPU:1, one launch (start us, length us, event | category | flops | bytes accessed | tf_op | source)
XLA Modules:
  0.0 70.0 jit_solution(3892609046484902546)
XLA Ops:
  0.0 2.1 %pack.1 = (f32[376,128]{1,0:T(8,128)}, f32[376,128]{1,0:T(8,128)}) custom-call(f32[1024,128]{1,0:T(8,128)} %perm_ref.3, s32[32,4,36]{2,1,0:T(4,128)} %sup_ref.3), custom_call_target="tpu_custom_call" | custom-call | tf_op jit(solution)/shard_map/pack/pallas_call | solution.py:61
  2.1 4.0 %collective-permute-start = (f32[376,128]{1,0:T(8,128)}, f32[376,128]{1,0:T(8,128)S(1)}, u32[]{:S(2)}, u32[]{:S(2)}) collective-permute-start(f32[376,128]{1,0:T(8,128)} %get-tuple-element.11), channel_id=1, source_target_pairs={{0,1},{1,2},{2,3},{4,5},{5,6},{6,7},{8,9},{9,10},{10,11},{12,13},{... | collective-permute-start | bytes 577544 | tf_op jit(solution)/shard_map/ppermute | solution.py:394
  6.1 1.3 %collective-permute-start.1 = (f32[376,128]{1,0:T(8,128)}, f32[376,128]{1,0:T(8,128)S(1)}, u32[]{:S(2)}, u32[]{:S(2)}) collective-permute-start(f32[376,128]{1,0:T(8,128)} %get-tuple-element.12), channel_id=1, source_target_pairs={{1,0},{2,1},{3,2},{5,4},{6,5},{7,6},{9,8},{10,9},{11,10},{13,12},{... | collective-permute-start | bytes 577544 | tf_op jit(solution)/shard_map/ppermute | solution.py:394
  7.4 2.5 %collective-permute-done.left_ref = f32[376,128]{1,0:T(8,128)S(1)} collective-permute-done((f32[376,128]{1,0:T(8,128)}, f32[376,128]{1,0:T(8,128)S(1)}, u32[]{:S(2)}, u32[]{:S(2)}) %collective-permute-start) | collective-permute-done | bytes 192544 | tf_op jit(solution)/shard_map/ppermute | solution.py:394
  9.9 0.0 copy-start
  9.9 3.7 %collective-permute-done.1.right_ref = f32[376,128]{1,0:T(8,128)S(1)} collective-permute-done((f32[376,128]{1,0:T(8,128)}, f32[376,128]{1,0:T(8,128)S(1)}, u32[]{:S(2)}, u32[]{:S(2)}) %collective-permute-start.1) | collective-permute-done | bytes 192544 | tf_op jit(solution)/shard_map/ppermute | solution.py:394
  13.6 0.0 copy-done
  13.6 0.0 copy-start.1
  13.6 0.7 copy-done.1
  14.2 2.9 %widen.1 = (f32[3,1024,128]{2,1,0:T(8,128)}, f32[10,32,128]{2,1,0:T(8,128)}, f32[120,128]{1,0:T(8,128)}, f32[120,128]{1,0:T(8,128)}) custom-call(f32[1024,128]{1,0:T(8,128)} %perm_ref.3, s32[32,4,36]{2,1,0:T(4,128)} %sup_ref.3, f32[376,128]{1,0:T(8,128)} %copy-done, f32[376,128]{1,0:T(8,128)} %copy-done.1), custom_call_target="tpu_custom_call" | custom-call | tf_op jit(solution)/shard_map/widen/pallas_call | solution.py:102
  17.2 4.9 %collective-permute-start.2 = (f32[120,128]{1,0:T(8,128)}, f32[120,128]{1,0:T(8,128)S(1)}, u32[]{:S(2)}, u32[]{:S(2)}) collective-permute-start(f32[120,128]{1,0:T(8,128)} %get-tuple-element.15), channel_id=1, source_target_pairs={{0,4},{4,8},{8,12},{1,5},{5,9},{9,13},{2,6},{6,10},{10,14},{3,7},{... | collective-permute-start | bytes 184328 | tf_op jit(solution)/shard_map/ppermute | solution.py:394
  22.1 1.9 %collective-permute-start.3 = (f32[120,128]{1,0:T(8,128)}, f32[120,128]{1,0:T(8,128)S(1)}, u32[]{:S(2)}, u32[]{:S(2)}) collective-permute-start(f32[120,128]{1,0:T(8,128)} %get-tuple-element.16), channel_id=1, source_target_pairs={{4,0},{8,4},{12,8},{5,1},{9,5},{13,9},{6,2},{10,6},{14,10},{7,3},{... | collective-permute-start | bytes 184328 | tf_op jit(solution)/shard_map/ppermute | solution.py:394
  24.0 0.0 collective-permute-done.2.low_ref
  24.0 0.0 copy-start.2
  24.0 3.8 %collective-permute-done.3.high_ref = f32[120,128]{1,0:T(8,128)S(1)} collective-permute-done((f32[120,128]{1,0:T(8,128)}, f32[120,128]{1,0:T(8,128)S(1)}, u32[]{:S(2)}, u32[]{:S(2)}) %collective-permute-start.3) | collective-permute-done | bytes 61472 | tf_op jit(solution)/shard_map/ppermute | solution.py:394
  27.8 0.0 copy-start.3
  27.8 0.0 copy-done.2
  27.8 0.6 copy-done.3
  28.4 41.6 %smooth.1 = f32[9216,128]{1,0:T(8,128)} custom-call(f32[3,1024,128]{2,1,0:T(8,128)} %get-tuple-element.13.field_hbm, f32[10,32,128]{2,1,0:T(8,128)} %get-tuple-element.14.sup_ref, f32[120,128]{1,0:T(8,128)} %copy-done.2, f32[120,128]{1,0:T(8,128)} %copy-done.3), custom_call_target="tpu_custom_call" | custom-call | tf_op jit(solution)/shard_map/smooth/pallas_call | solution.py:368
Async XLA Ops:
  2.1 7.8 %collective-permute-start = (f32[376,128]{1,0:T(8,128)}, f32[376,128]{1,0:T(8,128)S(1)}, u32[]{:S(2)}, u32[]{:S(2)}) collective-permute-start(f32[376,128]{1,0:T(8,128)} %get-tuple-element.11), channel_id=1, source_target_pairs={{0,1},{1,2},{2,3},{4,5},{5,6},{6,7},{8,9},{9,10},{10,11},{12,13},{... | collective-permute-start | bytes 577544 | tf_op jit(solution)/shard_map/ppermute | solution.py:394
  6.1 7.5 %collective-permute-start.1 = (f32[376,128]{1,0:T(8,128)}, f32[376,128]{1,0:T(8,128)S(1)}, u32[]{:S(2)}, u32[]{:S(2)}) collective-permute-start(f32[376,128]{1,0:T(8,128)} %get-tuple-element.12), channel_id=1, source_target_pairs={{1,0},{2,1},{3,2},{5,4},{6,5},{7,6},{9,8},{10,9},{11,10},{13,12},{... | collective-permute-start | bytes 577544 | tf_op jit(solution)/shard_map/ppermute | solution.py:394
  9.9 3.7 %copy-start = (f32[376,128]{1,0:T(8,128)}, f32[376,128]{1,0:T(8,128)S(1)}, u32[]{:S(2)}) copy-start(f32[376,128]{1,0:T(8,128)S(1)} %collective-permute-done.left_ref) | copy-start | bytes 577540
  13.6 0.7 copy-start.1
  17.2 6.8 %collective-permute-start.2 = (f32[120,128]{1,0:T(8,128)}, f32[120,128]{1,0:T(8,128)S(1)}, u32[]{:S(2)}, u32[]{:S(2)}) collective-permute-start(f32[120,128]{1,0:T(8,128)} %get-tuple-element.15), channel_id=1, source_target_pairs={{0,4},{4,8},{8,12},{1,5},{5,9},{9,13},{2,6},{6,10},{10,14},{3,7},{... | collective-permute-start | bytes 184328 | tf_op jit(solution)/shard_map/ppermute | solution.py:394
  22.1 5.8 %collective-permute-start.3 = (f32[120,128]{1,0:T(8,128)}, f32[120,128]{1,0:T(8,128)S(1)}, u32[]{:S(2)}, u32[]{:S(2)}) collective-permute-start(f32[120,128]{1,0:T(8,128)} %get-tuple-element.16), channel_id=1, source_target_pairs={{4,0},{8,4},{12,8},{5,1},{9,5},{13,9},{6,2},{10,6},{14,10},{7,3},{... | collective-permute-start | bytes 184328 | tf_op jit(solution)/shard_map/ppermute | solution.py:394
  24.0 3.8 %copy-start.2 = (f32[120,128]{1,0:T(8,128)}, f32[120,128]{1,0:T(8,128)S(1)}, u32[]{:S(2)}) copy-start(f32[120,128]{1,0:T(8,128)S(1)} %collective-permute-done.2.low_ref) | copy-start | bytes 184324
  27.8 0.6 copy-start.3

commit v3 on v2

v3 whole, which is shorter than its diff:
```python
import functools

import jax
import jax.numpy as jnp
from jax import lax
from jax.experimental import pallas as pl
from jax.experimental.pallas import tpu as pltpu
from jax.sharding import PartitionSpec as P

ITERS = 4
SIDES = (-1, 0, 1)
TINY = 1e-30
OFF = 2.0

RIM = 4
PAD = 8
HIGH = 32 + 2 * RIM
PITCH = 64 + 2 * PAD
BANDS = 3
LANE_PITCH = 40
HALO = 40
WIDTH = 32 + RIM
FIELD_ROWS = 32 * LANE_PITCH + 16
SUP_PITCH = 48
BLOCK_ROWS = 36 * 8

f32 = jnp.float32


def cost(amount):
    return pl.CostEstimate(flops=amount, bytes_accessed=amount, transcendentals=0)


def support_rows(sup_ref):
    pad = jnp.zeros((sup_ref.shape[0], 92), f32)
    return [jnp.concatenate([sup_ref[:, q, :].astype(f32), pad], axis=1) for q in range(4)]


def groups_of(rows):
    third = -(-rows // 24) * 8
    return [(g, g * third, min(third, rows - g * third)) for g in range(3)]


def pack_kernel(perm_ref, sup_ref, up_ref, down_ref):
    rows = perm_ref.shape[0]
    parts = groups_of(rows)
    third = parts[0][2]
    lane = lax.broadcasted_iota(jnp.int32, (third, 128), 1)
    up = down = None
    for g, start, count in parts:
        part = perm_ref[start : start + count, :]
        if count < third:
            part = jnp.concatenate([part, jnp.zeros((third - count, 128), f32)], axis=0)
        high = pltpu.roll(part, WIDTH * (g + 1), 1)
        low = part if g == 0 else pltpu.roll(part, WIDTH * g, 1)
        up = high if up is None else jnp.where(lane < WIDTH * g, up, high)
        down = low if down is None else jnp.where(lane < WIDTH * g, down, low)
    up_ref[:third, :] = up
    down_ref[:third, :] = down
    wide = support_rows(sup_ref)
    up_ref[third:, :] = wide[1] + pltpu.roll(wide[2], 36, 1) + pltpu.roll(wide[3], 72, 1)
    down_ref[third:, :] = wide[0] + pltpu.roll(wide[1], 36, 1) + pltpu.roll(wide[2], 72, 1)


def pack(perm, support):
    third = groups_of(perm.shape[0])[0][2]
    shape = jax.ShapeDtypeStruct((third + support.shape[0], 128), f32)
    return pl.pallas_call(pack_kernel, out_shape=(shape, shape), name="pack")(perm, support)


def bands_of(own, left, right, g):
    lane = lax.broadcasted_iota(jnp.int32, own.shape, 1)
    moved = pltpu.roll(own, WIDTH, 1)
    if g > 0:
        left = pltpu.roll(left, 128 - WIDTH * g, 1)
    if g != 1:
        right = pltpu.roll(right, (128 + WIDTH - WIDTH * g) % 128, 1)
    return (
        jnp.where(lane < WIDTH, left, moved),
        pltpu.roll(own, 64 + WIDTH, 1),
        jnp.where(lane < WIDTH, moved, jnp.where(lane < 2 * WIDTH, right, 0.0)),
    )


def wide_support(sup_ref, left, right):
    shift = [0, 128 - 36, 128 - 72]
    low = [pltpu.roll(left, by, 1) if by else left for by in shift]
    high = [pltpu.roll(right, by, 1) if by else right for by in shift]
    return low + support_rows(sup_ref) + high


def edge_kernel(perm_ref, sup_ref, left_ref, right_ref, up_ref, down_ref):
    rows, blocks = perm_ref.shape[0], sup_ref.shape[0]
    groups = groups_of(rows)
    third = groups[0][2]
    for ref, g, start, block in ((up_ref, 2, rows - HALO, blocks - 4), (down_ref, 0, 0, 0)):
        packed = slice(start - groups[g][1], start - groups[g][1] + HALO)
        bands = bands_of(perm_ref[start : start + HALO, :], left_ref[packed, :], right_ref[packed, :], g)
        ref[:HALO, :] = bands[0]
        ref[HALO : 2 * HALO, :] = bands[2]
        four = slice(third + block, third + block + 4)
        wide = wide_support(sup_ref.at[pl.ds(block, 4)], left_ref[four, :], right_ref[four, :])
        for q in range(10):
            ref[2 * HALO + 4 * q : 2 * HALO + 4 * q + 4, :] = wide[q]


def edges(perm, support, from_left, from_right):
    edge = jax.ShapeDtypeStruct((2 * HALO + 40, 128), f32)
    return pl.pallas_call(
        edge_kernel, out_shape=(edge, edge), cost_estimate=cost(100_000), name="edges"
    )(perm, support, from_left, from_right)


def widen_kernel(perm_ref, sup_ref, left_ref, right_ref, field_ref, wide_ref):
    rows = perm_ref.shape[0]
    groups = groups_of(rows)
    third = groups[0][2]
    for g, start, count in groups:
        bands = bands_of(
            perm_ref[start : start + count, :], left_ref[:count, :], right_ref[:count, :], g
        )
        for band in range(BANDS):
            field_ref[band, start : start + count, :] = bands[band]
    for q, wide in enumerate(wide_support(sup_ref, left_ref[third:, :], right_ref[third:, :])):
        wide_ref[q] = wide


def widen(perm, support, from_left, from_right):
    rows, blocks = perm.shape[0], support.shape[0]
    return pl.pallas_call(
        widen_kernel,
        out_shape=(
            jax.ShapeDtypeStruct((BANDS, rows, 128), f32),
            jax.ShapeDtypeStruct((10, blocks, 128), f32),
        ),
        cost_estimate=cost(4_000_000),
        name="widen",
    )(perm, support, from_left, from_right)


def build_cells(field, cells):
    blank = jnp.zeros((128 - BANDS * LANE_PITCH, 128), f32)
    edge = jnp.zeros((PAD - RIM, 128), f32)

    def row(step, carry):
        for u in range(10):
            x = 10 * step + u
            parts = [
                field[pl.ds(band * FIELD_ROWS + 256 * m + x + HALO - WIDTH, 8, stride=32), :]
                for band in range(BANDS)
                for m in range(LANE_PITCH // 8)
            ]
            turned = jnp.concatenate(parts + [blank], axis=0).T
            cells[x, 0 : PAD - RIM, :] = edge
            cells[x, PAD - RIM : PITCH - PAD + RIM, :] = turned[: 64 + 2 * RIM]
            cells[x, PITCH - PAD + RIM : PITCH, :] = edge
        return carry

    lax.fori_loop(0, HIGH // 10, row, 0)


PIECES = (
    (PAD - RIM, RIM, 0, 1),
    (PAD, 16, 1, 0),
    (PAD + 16, 16, 1, 1),
    (PAD + 32, 16, 2, 0),
    (PAD + 48, 16, 2, 1),
    (PAD + 64, RIM, 3, 0),
)


def side_of(label, region):
    return (label - region + 1) % 3 - 1


def build_masks(cells, sup, turned, mask):
    blank = jnp.zeros((128 - BANDS * LANE_PITCH, 128), f32)
    for ex in range(5):
        for ey in range(6):
            parts = [
                sup[(2 * band + ey) * SUP_PITCH + ex : (2 * band + ey) * SUP_PITCH + ex + LANE_PITCH, :]
                for band in range(BANDS)
            ]
            turned[ex, ey] = jnp.concatenate(parts + [blank], axis=0).T[:40]
    for tile, (x, rx, tr) in enumerate(
        ((RIM - 1, 0, 1), (RIM, 1, 0), (RIM + 16, 1, 1), (RIM + 32, 2, 0))
    ):
        for start, count, region, tc in PIECES:
            inside = cells[x, start : start + 1, :] > 0.0
            for dx in SIDES:
                for label in range(3):
                    dy = side_of(label, region)
                    if dx == 0 and dy == 0:
                        on = inside
                    else:
                        t = 6 * (2 * (1 - dx) + tr) + 2 * (1 - dy) + tc
                        on = inside & (turned[rx + dx + 1, region + dy + 1, t : t + 1, :] == 1.0)
                    mask[tile, 3 * (dx + 1) + label, start : start + count, :] = jnp.broadcast_to(
                        jnp.where(on, f32(1.0), f32(0.0)), (count, 128)
                    )


def build_faces(cells, coef):
    starts = [PAD - RIM + 8 * m for m in range(9)]
    zero = jnp.zeros((8, 128), f32)
    sub = lax.broadcasted_iota(jnp.int32, (8, 128), 0)

    def face(p, q):
        return 2.0 * p * q / jnp.maximum(p + q, TINY)

    def row(x, west):
        east, south = [], []
        for z in starts:
            here = cells[x, z : z + 8, :]
            east.append(face(here, cells[x + 1, z : z + 8, :]))
            south.append(face(here, cells[x, z - 1 : z + 7, :]))
        for m, z in enumerate(starts):
            after = south[m + 1] if m < 8 else zero
            north = jnp.where(sub == 7, pltpu.roll(after, 7, 0), pltpu.roll(south[m], 7, 0))
            scale = OFF / jnp.maximum(west[m] + east[m] + south[m] + north, TINY)
            coef[0, x, z : z + 8, :] = scale * west[m]
            coef[1, x, z : z + 8, :] = scale * east[m]
            coef[2, x, z : z + 8, :] = scale * south[m]
            coef[3, x, z : z + 8, :] = scale * north
        return tuple(east)

    first = tuple(face(cells[0, z : z + 8, :], cells[1, z : z + 8, :]) for z in starts)
    lax.fori_loop(1, HIGH - 1, row, first)


def cut(field, z, edge):
    if not z <= edge < z + 8:
        return field
    sub = lax.broadcasted_iota(jnp.int32, (8, 128), 0)
    return jnp.where(sub == edge - z, 0.0, field)


EDGES = (PAD + 32, PAD + 64, PAD)


def region_of(z):
    return 0 if z < PAD else 3 if z >= PAD + 64 else 1 + (z - PAD) // 32


def finish(terms, new, mask, x, tile, rows):
    total = None
    for at, term in enumerate(terms):
        if term is not None:
            terms[at] = term = mask[tile, at, rows, :] * term
            total = term if total is None else total + term
    inverse = 1.0 / jnp.maximum(total, TINY)
    for at, term in enumerate(terms):
        new[at, x, rows, :] = jnp.zeros((8, 128), f32) if term is None else term * inverse


def where_own(label, z, value):
    own = [side_of(label, region_of(z + i)) == 0 for i in range(8)]
    if all(own):
        return value
    if not any(own):
        return None
    sub = lax.broadcasted_iota(jnp.int32, (8, 128), 0)
    first, count = own.index(True), sum(own)
    return jnp.where((sub >= first) & (sub < first + count), value, 0.0)


def add(a, b):
    return b if a is None else a if b is None else a + b


def first_vector(new, coef, mask, x, tile, z, first_row, last_row):
    rows = slice(z, z + 8)
    west, east = coef[0, x, rows, :], coef[1, x, rows, :]
    south, north = coef[2, x, rows, :], coef[3, x, rows, :]
    middle = jnp.ones((8, 128), f32)
    middle = middle if first_row else middle + west
    middle = middle if last_row else middle + east
    terms = [None] * 9
    for label in range(3):
        term = where_own(label, z, middle)
        term = add(term, where_own(label, z - 1, cut(south, z, EDGES[label])))
        terms[3 + label] = add(term, where_own(label, z + 1, cut(north, z, EDGES[label] - 1)))
        if first_row:
            terms[label] = where_own(label, z, west)
        if last_row:
            terms[6 + label] = where_own(label, z, east)
    finish(terms, new, mask, x, tile, rows)


def smooth_vector(old, new, coef, mask, x, tile, z, first_row, last_row):
    rows = slice(z, z + 8)
    west, east = coef[0, x, rows, :], coef[1, x, rows, :]
    south, north = coef[2, x, rows, :], coef[3, x, rows, :]
    souths = [cut(south, z, edge) for edge in EDGES]
    norths = [cut(north, z, edge - 1) for edge in EDGES]
    terms = []
    for dx in SIDES:
        for label in range(3):
            at = 3 * (dx + 1) + label
            term = old[at, x, rows, :]
            if not first_row:
                term = term + west * old[at, x - 1, rows, :]
            elif dx < 1:
                term = term + west * old[at + 3, x - 1, rows, :]
            if not last_row:
                term = term + east * old[at, x + 1, rows, :]
            elif dx > -1:
                term = term + east * old[at - 3, x + 1, rows, :]
            term = term + souths[label] * old[at, x, z - 1 : z + 7, :]
            term = term + norths[label] * old[at, x, z + 1 : z + 9, :]
            terms.append(term)
    finish(terms, new, mask, x, tile, rows)


def iterate(vector, rim):
    def row(x, tile, first_row=False, last_row=False):
        for m in range(9):
            vector(x, tile, PAD - RIM + 8 * m, first_row, last_row)

    def rows(begin, end, tile):
        def step(x, carry):
            row(x, tile)
            return carry

        lax.fori_loop(begin, end, step, 0)

    rows(RIM - rim, RIM - 1, 0)
    row(RIM - 1, 0, last_row=True)
    row(RIM, 1, first_row=True)

    def inner(x, carry):
        row(x, jnp.where(x < RIM + 16, 1, 2))
        return carry

    lax.fori_loop(RIM + 1, RIM + 31, inner, 0)
    row(RIM + 31, 2, last_row=True)
    row(RIM + 32, 3, first_row=True)
    rows(RIM + 33, RIM + 32 + rim, 3)


def turn_tile(values, staged, part, dx, label, tc):
    z = PAD + 16 * tc
    region = 1 + tc // 2
    dy = side_of(label, region)
    cells = [values[3 * (dx + 1) + label, RIM + 8 * part + u, z : z + 16, :] for u in range(8)]
    turned = jnp.concatenate(cells, axis=0).T
    t = 6 * (2 * (1 - dx) + part // 2) + 2 * (1 - dy) + tc % 2
    for band in range(BANDS):
        q = 2 * band - 2 + region + dy
        if 0 <= q < 4:
            at = (8 * t + 4 * (part % 2) + q) * LANE_PITCH
            staged[at : at + LANE_PITCH, :] = turned[LANE_PITCH * band : LANE_PITCH * (band + 1)]


def gather_tiles(staged, out, blocks, tr):
    def block(p, carry):
        for side in range(3):
            for b in range(6):
                t = 6 * (2 * side + tr) + b
                out[p, side, tr, 8 * b : 8 * b + 8, :] = staged[
                    pl.ds(8 * t * LANE_PITCH + p + side, 8, stride=LANE_PITCH), :
                ]
        return carry

    lax.fori_loop(0, blocks, block, 0)


def last_iteration(old, new, coef, mask, staged, out, out_hbm, sem, blocks):
    jobs = [(dx, label, tc) for dx in SIDES for label in range(3) for tc in range(4)]
    copies = []
    for part in range(5):
        if part < 4:
            for u in range(8):
                x = RIM + 8 * part + u
                for m in range(8):
                    smooth_vector(
                        old, new, coef, mask, x, 1 + part // 2, PAD + 8 * m, x == RIM, x == RIM + 31
                    )
                if part > 0:
                    for job in jobs[36 * u // 8 : 36 * (u + 1) // 8]:
                        turn_tile(new, staged, part - 1, *job)
        else:
            for job in jobs:
                turn_tile(new, staged, part - 1, *job)
        if part in (2, 4):
            tr = part // 2 - 1
            gather_tiles(staged, out, blocks, tr)
            copy = pltpu.make_async_copy(out.at[:, :, tr], out_hbm.at[:, :, tr], sem.at[tr])
            copy.start()
            copies.append(copy)
    for copy in copies:
        copy.wait()


def main_kernel(
    field_hbm, sup_ref, low_ref, high_ref, out_hbm,
    field, sup, cells, turned, mask, coef, values, other, staged, out, sem,
):
    rows = field_hbm.shape[1]
    blocks = sup_ref.shape[1]
    copies = []
    for band in range(BANDS):
        copy = pltpu.make_async_copy(
            field_hbm.at[band],
            field.at[pl.ds(band * FIELD_ROWS + HALO, rows), :],
            sem.at[band],
        )
        copy.start()
        copies.append(copy)
    lane = lax.broadcasted_iota(jnp.int32, (HALO, 128), 1)
    for ref, at in ((low_ref, 0), (high_ref, HALO + rows)):
        left, right = ref[:HALO, :], ref[HALO : 2 * HALO, :]
        field[at : at + HALO, :] = left
        at = at + FIELD_ROWS
        field[at : at + HALO, :] = jnp.where(lane < 64, pltpu.roll(left, 64, 1), pltpu.roll(right, 64, 1))
        at = at + FIELD_ROWS
        field[at : at + HALO, :] = right
    rest = FIELD_ROWS - rows - 2 * HALO
    for band in range(BANDS):
        at = band * FIELD_ROWS + rows + 2 * HALO
        field[at : at + rest, :] = jnp.zeros((rest, 128), f32)
    for q in range(10):
        at = q * SUP_PITCH
        sup[at : at + 3, :] = low_ref[2 * HALO + 4 * q + 1 : 2 * HALO + 4 * q + 4, :]
        sup[at + 3 : at + 3 + blocks, :] = sup_ref[q]
        sup[at + 3 + blocks : at + 6 + blocks, :] = high_ref[2 * HALO + 4 * q : 2 * HALO + 4 * q + 3, :]
        sup[at + 6 + blocks : at + SUP_PITCH, :] = jnp.zeros((SUP_PITCH - 6 - blocks, 128), f32)
    for copy in copies:
        copy.wait()
    build_cells(field, cells)
    build_masks(cells, sup, turned, mask)
    build_faces(cells, coef)
    iterate(functools.partial(first_vector, other, coef, mask), ITERS - 1)
    old, new = other, values
    for count in range(1, ITERS - 1):
        iterate(functools.partial(smooth_vector, old, new, coef, mask), ITERS - 1 - count)
        old, new = new, old
    last_iteration(old, new, coef, mask, staged, out, out_hbm, sem, blocks)


def smooth(field, sup, low, high):
    blocks = sup.shape[1]
    vmem = pl.BlockSpec(memory_space=pltpu.VMEM)
    hbm = pl.BlockSpec(memory_space=pl.ANY)
    return pl.pallas_call(
        main_kernel,
        out_shape=jax.ShapeDtypeStruct((blocks, 3, 2, 48, 128), f32),
        in_specs=[hbm, vmem, vmem, vmem],
        out_specs=hbm,
        scratch_shapes=[
            pltpu.VMEM((BANDS * FIELD_ROWS, 128), f32),
            pltpu.VMEM((10 * SUP_PITCH, 128), f32),
            pltpu.VMEM((HIGH, PITCH, 128), f32),
            pltpu.VMEM((5, 6, 40, 128), f32),
            pltpu.VMEM((4, 9, PITCH, 128), f32),
            pltpu.VMEM((4, HIGH, PITCH, 128), f32),
            pltpu.VMEM((9, HIGH, PITCH, 128), f32),
            pltpu.VMEM((9, HIGH, PITCH, 128), f32),
            pltpu.VMEM((LANE_PITCH * BLOCK_ROWS, 128), f32),
            pltpu.VMEM((blocks, 3, 2, 48, 128), f32),
            pltpu.SemaphoreType.DMA((BANDS,)),
        ],
        compiler_params=pltpu.CompilerParams(vmem_limit_bytes=60 * 1024 * 1024),
        name="smooth",
    )(field, sup, low, high)


def neighbours(up, down, axis):
    count = lax.axis_size(axis)
    forward = [(i, i + 1) for i in range(count - 1)]
    backward = [(i + 1, i) for i in range(count - 1)]
    return lax.ppermute(up, axis, forward), lax.ppermute(down, axis, backward)


def body(permeability, support):
    up, down = pack(permeability, support)
    from_left, from_right = neighbours(up, down, "gy")
    up, down = edges(permeability, support, from_left, from_right)
    low, high = neighbours(up, down, "gx")
    field, sup = widen(permeability, support, from_left, from_right)
    tiles = smooth(field, sup, low, high).reshape(support.shape[0], 36, 2, 4, 128)
    return tiles.transpose(0, 3, 1, 2, 4).reshape(support.shape + (256,))


def solution(mesh):
    return jax.shard_map(
        body,
        mesh=mesh,
        in_specs=(P(("grp", "gx"), "gy"), P(("grp", "gx"), "gy", None)),
        out_specs=P(("grp", "gx"), "gy", None, None),
        check_vma=False,
    )
```

time: 70.3 us -> 56.9 us (0.81)
  Pallas kernels: 46.6 us -> 36.1 us
  waiting for transfers between devices: 9.97 us -> 7.04 us
    pallas_call x1 -> x2, Pallas kernels: 41.6 us -> 31.1 us  [the longest x1 29.2 us: smooth(): pl.pallas_call(main_kernel, out_shape=jax.ShapeDtypeStruct((blocks, 3, 2,...]
    ppermute x4, waiting for transfers between devices: 9.97 us -> 7.04 us  [neighbours(): return (lax.ppermute(up, axis, forward), lax.ppermute(down, axis, backward))]
  transfers between devices with their start and end apart: 4 -> 4, of which waited for: 3 -> 3; matrix products, arithmetic and copies ran while one was open for 0% -> 0% of each run, Pallas kernels for 0% -> 5%
where the time goes in v3:
time: 56.9 us; the launch traced here: 56.6 us
  Pallas kernels  36.1 us (63%)
  starting transfers between devices  12.1 us (21%)
  waiting for transfers between devices  7.04 us (12%)
  local copies, waits for them, and re-layouts  1.3 us (2%)
    pallas_call x1, Pallas kernels, smooth(): pl.pallas_call(main_kernel, out_shape=jax.ShapeDtypeStruct((blocks, 3, 2,...  29.2 us
    ppermute x4, starting transfers between devices, neighbours(): return (lax.ppermute(up, axis, forward), lax.ppermute(down, axis, backward))  12.1 us
    ppermute x4, waiting for transfers between devices, neighbours(): return (lax.ppermute(up, axis, forward), lax.ppermute(down, axis, backward))  7.04 us
    pallas_call x1, Pallas kernels, widen(): pl.pallas_call(widen_kernel, out_shape=(jax.ShapeDtypeStruct((BANDS, rows...  2.94 us
    pallas_call x1, Pallas kernels, pack(): pl.pallas_call(pack_kernel, out_shape=(shape, shape), name='pack')  2.06 us
    pallas_call x1, Pallas kernels, edges(): pl.pallas_call(edge_kernel, out_shape=(edge, edge), cost_estimate=cost(10...  1.93 us
    unnamed x8, local copies, waits for them, and re-layouts  1.3 us
  transfers between devices with their start and end apart: 4, of which 3 were waited for; matrix products, arithmetic and copies ran while one was open for 0% of the time, Pallas kernels for 5%

profile of v3, /device:TPU:1, one launch (start us, length us, event | category | flops | bytes accessed | tf_op | source)
XLA Modules:
  0.0 56.6 jit_solution(10167137493784403306)
XLA Ops:
  0.0 2.1 %pack.1 = (f32[376,128]{1,0:T(8,128)}, f32[376,128]{1,0:T(8,128)}) custom-call(f32[1024,128]{1,0:T(8,128)} %perm_ref.5, s32[32,4,36]{2,1,0:T(4,128)} %sup_ref.5), custom_call_target="tpu_custom_call" | custom-call | tf_op jit(solution)/shard_map/pack/pallas_call | solution.py:68
  2.1 4.0 %collective-permute-start = (f32[376,128]{1,0:T(8,128)}, f32[376,128]{1,0:T(8,128)S(1)}, u32[]{:S(2)}, u32[]{:S(2)}) collective-permute-start(f32[376,128]{1,0:T(8,128)} %get-tuple-element.11), channel_id=1, source_target_pairs={{0,1},{1,2},{2,3},{4,5},{5,6},{6,7},{8,9},{9,10},{10,11},{12,13},{... | collective-permute-start | bytes 577544 | tf_op jit(solution)/shard_map/ppermute | solution.py:472
  6.1 1.3 %collective-permute-start.1 = (f32[376,128]{1,0:T(8,128)}, f32[376,128]{1,0:T(8,128)S(1)}, u32[]{:S(2)}, u32[]{:S(2)}) collective-permute-start(f32[376,128]{1,0:T(8,128)} %get-tuple-element.12), channel_id=1, source_target_pairs={{1,0},{2,1},{3,2},{5,4},{6,5},{7,6},{9,8},{10,9},{11,10},{13,12},{... | collective-permute-start | bytes 577544 | tf_op jit(solution)/shard_map/ppermute | solution.py:472
  7.4 2.5 %collective-permute-done.left_ref = f32[376,128]{1,0:T(8,128)S(1)} collective-permute-done((f32[376,128]{1,0:T(8,128)}, f32[376,128]{1,0:T(8,128)S(1)}, u32[]{:S(2)}, u32[]{:S(2)}) %collective-permute-start) | collective-permute-done | bytes 192544 | tf_op jit(solution)/shard_map/ppermute | solution.py:472
  9.9 0.0 copy-start
  9.9 3.7 %collective-permute-done.1.right_ref = f32[376,128]{1,0:T(8,128)S(1)} collective-permute-done((f32[376,128]{1,0:T(8,128)}, f32[376,128]{1,0:T(8,128)S(1)}, u32[]{:S(2)}, u32[]{:S(2)}) %collective-permute-start.1) | collective-permute-done | bytes 192544 | tf_op jit(solution)/shard_map/ppermute | solution.py:472
  13.6 0.0 copy-done
  13.6 0.0 copy-start.1
  13.6 0.7 %copy-done.1 = f32[376,128]{1,0:T(8,128)} copy-done((f32[376,128]{1,0:T(8,128)}, f32[376,128]{1,0:T(8,128)S(1)}, u32[]{:S(2)}) %copy-start.1) | copy-done | bytes 192536
  14.2 1.9 %edges.1 = (f32[120,128]{1,0:T(8,128)}, f32[120,128]{1,0:T(8,128)}) custom-call(f32[1024,128]{1,0:T(8,128)} %perm_ref.5, s32[32,4,36]{2,1,0:T(4,128)} %sup_ref.5, f32[376,128]{1,0:T(8,128)} %copy-done, f32[376,128]{1,0:T(8,128)} %copy-done.1), custom_call_target="tpu_custom_call" | custom-call | flops 100000 | bytes 100000 | tf_op jit(solution)/shard_map/edges/pallas_call | solution.py:109
  16.2 4.9 %collective-permute-start.2 = (f32[120,128]{1,0:T(8,128)}, f32[120,128]{1,0:T(8,128)S(1)}, u32[]{:S(2)}, u32[]{:S(2)}) collective-permute-start(f32[120,128]{1,0:T(8,128)} %get-tuple-element.15), channel_id=1, source_target_pairs={{0,4},{4,8},{8,12},{1,5},{5,9},{9,13},{2,6},{6,10},{10,14},{3,7},{... | collective-permute-start | bytes 184328 | tf_op jit(solution)/shard_map/ppermute | solution.py:472
  21.0 1.9 %collective-permute-start.3 = (f32[120,128]{1,0:T(8,128)}, f32[120,128]{1,0:T(8,128)S(1)}, u32[]{:S(2)}, u32[]{:S(2)}) collective-permute-start(f32[120,128]{1,0:T(8,128)} %get-tuple-element.16), channel_id=1, source_target_pairs={{4,0},{8,4},{12,8},{5,1},{9,5},{13,9},{6,2},{10,6},{14,10},{7,3},{... | collective-permute-start | bytes 184328 | tf_op jit(solution)/shard_map/ppermute | solution.py:472
  23.0 2.9 %widen.1 = (f32[3,1024,128]{2,1,0:T(8,128)}, f32[10,32,128]{2,1,0:T(8,128)}) custom-call(f32[1024,128]{1,0:T(8,128)} %perm_ref.5, s32[32,4,36]{2,1,0:T(4,128)} %sup_ref.5, f32[376,128]{1,0:T(8,128)} %copy-done, f32[376,128]{1,0:T(8,128)} %copy-done.1), custom_call_target="tpu_custom_call" | custom-call | flops 4000000 | bytes 4000000 | tf_op jit(solution)/shard_map/widen/pallas_call | solution.py:130
  25.9 0.0 collective-permute-done.2.low_ref
  25.9 0.0 copy-start.2
  25.9 0.9 %collective-permute-done.3.high_ref = f32[120,128]{1,0:T(8,128)S(1)} collective-permute-done((f32[120,128]{1,0:T(8,128)}, f32[120,128]{1,0:T(8,128)S(1)}, u32[]{:S(2)}, u32[]{:S(2)}) %collective-permute-start.3) | collective-permute-done | bytes 61472 | tf_op jit(solution)/shard_map/ppermute | solution.py:472
  26.8 0.0 copy-start.3
  26.8 0.0 copy-done.2
  26.8 0.6 %copy-done.3 = f32[120,128]{1,0:T(8,128)} copy-done((f32[120,128]{1,0:T(8,128)}, f32[120,128]{1,0:T(8,128)S(1)}, u32[]{:S(2)}) %copy-start.3) | copy-done | bytes 61464
  27.4 29.2 %smooth.1 = f32[32,3,2,48,128]{4,3,2,1,0:T(8,128)} custom-call(f32[3,1024,128]{2,1,0:T(8,128)} %get-tuple-element.13.field_hbm, f32[10,32,128]{2,1,0:T(8,128)} %get-tuple-element.14.sup_ref, f32[120,128]{1,0:T(8,128)} %copy-done.2, f32[120,128]{1,0:T(8,128)} %copy-done.3), custom_call_target="tpu_custom_call" | custom-call | tf_op jit(solution)/shard_map/smooth/pallas_call | solution.py:445
Async XLA Ops:
  2.1 7.8 %collective-permute-start = (f32[376,128]{1,0:T(8,128)}, f32[376,128]{1,0:T(8,128)S(1)}, u32[]{:S(2)}, u32[]{:S(2)}) collective-permute-start(f32[376,128]{1,0:T(8,128)} %get-tuple-element.11), channel_id=1, source_target_pairs={{0,1},{1,2},{2,3},{4,5},{5,6},{6,7},{8,9},{9,10},{10,11},{12,13},{... | collective-permute-start | bytes 577544 | tf_op jit(solution)/shard_map/ppermute | solution.py:472
  6.1 7.5 %collective-permute-start.1 = (f32[376,128]{1,0:T(8,128)}, f32[376,128]{1,0:T(8,128)S(1)}, u32[]{:S(2)}, u32[]{:S(2)}) collective-permute-start(f32[376,128]{1,0:T(8,128)} %get-tuple-element.12), channel_id=1, source_target_pairs={{1,0},{2,1},{3,2},{5,4},{6,5},{7,6},{9,8},{10,9},{11,10},{13,12},{... | collective-permute-start | bytes 577544 | tf_op jit(solution)/shard_map/ppermute | solution.py:472
  9.9 3.7 %copy-start = (f32[376,128]{1,0:T(8,128)}, f32[376,128]{1,0:T(8,128)S(1)}, u32[]{:S(2)}) copy-start(f32[376,128]{1,0:T(8,128)S(1)} %collective-permute-done.left_ref) | copy-start | bytes 577540
  13.6 0.7 %copy-start.1 = (f32[376,128]{1,0:T(8,128)}, f32[376,128]{1,0:T(8,128)S(1)}, u32[]{:S(2)}) copy-start(f32[376,128]{1,0:T(8,128)S(1)} %collective-permute-done.1.right_ref) | copy-start | bytes 577540
  16.2 9.7 %collective-permute-start.2 = (f32[120,128]{1,0:T(8,128)}, f32[120,128]{1,0:T(8,128)S(1)}, u32[]{:S(2)}, u32[]{:S(2)}) collective-permute-start(f32[120,128]{1,0:T(8,128)} %get-tuple-element.15), channel_id=1, source_target_pairs={{0,4},{4,8},{8,12},{1,5},{5,9},{9,13},{2,6},{6,10},{10,14},{3,7},{... | collective-permute-start | bytes 184328 | tf_op jit(solution)/shard_map/ppermute | solution.py:472
  21.0 5.8 %collective-permute-start.3 = (f32[120,128]{1,0:T(8,128)}, f32[120,128]{1,0:T(8,128)S(1)}, u32[]{:S(2)}, u32[]{:S(2)}) collective-permute-start(f32[120,128]{1,0:T(8,128)} %get-tuple-element.16), channel_id=1, source_target_pairs={{4,0},{8,4},{12,8},{5,1},{9,5},{13,9},{6,2},{10,6},{14,10},{7,3},{... | collective-permute-start | bytes 184328 | tf_op jit(solution)/shard_map/ppermute | solution.py:472
  25.9 0.9 %copy-start.2 = (f32[120,128]{1,0:T(8,128)}, f32[120,128]{1,0:T(8,128)S(1)}, u32[]{:S(2)}) copy-start(f32[120,128]{1,0:T(8,128)S(1)} %collective-permute-done.2.low_ref) | copy-start | bytes 184324
  26.8 0.6 %copy-start.3 = (f32[120,128]{1,0:T(8,128)}, f32[120,128]{1,0:T(8,128)S(1)}, u32[]{:S(2)}) copy-start(f32[120,128]{1,0:T(8,128)S(1)} %collective-permute-done.3.high_ref) | copy-start | bytes 184324

commit v4 on v3

--- a/solution.py
+++ b/solution.py
@@ -173,7 +173,7 @@
     return (label - region + 1) % 3 - 1
 
 
-def build_masks(cells, sup, turned, mask):
+def turn_support(sup, turned):
     blank = jnp.zeros((128 - BANDS * LANE_PITCH, 128), f32)
     for ex in range(5):
         for ey in range(6):
@@ -182,6 +182,9 @@
                 for band in range(BANDS)
             ]
             turned[ex, ey] = jnp.concatenate(parts + [blank], axis=0).T[:40]
+
+
+def build_masks(cells, turned, mask):
     for tile, (x, rx, tr) in enumerate(
         ((RIM - 1, 0, 1), (RIM, 1, 0), (RIM + 16, 1, 1), (RIM + 32, 2, 0))
     ):
@@ -352,17 +355,19 @@
             staged[at : at + LANE_PITCH, :] = turned[LANE_PITCH * band : LANE_PITCH * (band + 1)]
 
 
-def gather_tiles(staged, out, blocks, tr):
-    def block(p, carry):
-        for side in range(3):
-            for b in range(6):
-                t = 6 * (2 * side + tr) + b
-                out[p, side, tr, 8 * b : 8 * b + 8, :] = staged[
-                    pl.ds(8 * t * LANE_PITCH + p + side, 8, stride=LANE_PITCH), :
-                ]
+def gather_tiles(staged, out, begin, end, tr):
+    def block(step, carry):
+        for u in range(4):
+            p = 4 * step + u
+            for side in range(3):
+                for b in range(6):
+                    t = 6 * (2 * side + tr) + b
+                    out[p, side, tr, 8 * b : 8 * b + 8, :] = staged[
+                        pl.ds(8 * t * LANE_PITCH + p + side, 8, stride=LANE_PITCH), :
+                    ]
         return carry
 
-    lax.fori_loop(0, blocks, block, 0)
+    lax.fori_loop(begin // 4, end // 4, block, 0)
 
 
 def last_iteration(old, new, coef, mask, staged, out, out_hbm, sem, blocks):
@@ -384,10 +389,14 @@
                 turn_tile(new, staged, part - 1, *job)
         if part in (2, 4):
             tr = part // 2 - 1
-            gather_tiles(staged, out, blocks, tr)
-            copy = pltpu.make_async_copy(out.at[:, :, tr], out_hbm.at[:, :, tr], sem.at[tr])
-            copy.start()
-            copies.append(copy)
+            for side in range(2):
+                begin, end = side * blocks // 2, (side + 1) * blocks // 2
+                gather_tiles(staged, out, begin, end, tr)
+                copy = pltpu.make_async_copy(
+                    out.at[begin:end, :, tr], out_hbm.at[begin:end, :, tr], sem.at[2 * tr + side]
+                )
+                copy.start()
+                copies.append(copy)
     for copy in copies:
         copy.wait()
 
@@ -398,15 +407,22 @@
 ):
     rows = field_hbm.shape[1]
     blocks = sup_ref.shape[1]
-    copies = []
+    copies = [
+        pltpu.make_async_copy(
+            field_hbm.at[band], field.at[pl.ds(band * FIELD_ROWS + HALO, rows), :], sem.at[band]
+        )
+        for band in range(BANDS)
+    ]
+    for copy in copies:
+        copy.start()
+    for q in range(10):
+        at = q * SUP_PITCH
+        sup[at + 3 : at + 3 + blocks, :] = sup_ref[q]
+        sup[at + 6 + blocks : at + SUP_PITCH, :] = jnp.zeros((SUP_PITCH - 6 - blocks, 128), f32)
+    rest = FIELD_ROWS - rows - 2 * HALO
     for band in range(BANDS):
-        copy = pltpu.make_async_copy(
-            field_hbm.at[band],
-            field.at[pl.ds(band * FIELD_ROWS + HALO, rows), :],
-            sem.at[band],
-        )
-        copy.start()
-        copies.append(copy)
+        at = band * FIELD_ROWS + rows + 2 * HALO
+        field[at : at + rest, :] = jnp.zeros((rest, 128), f32)
     lane = lax.broadcasted_iota(jnp.int32, (HALO, 128), 1)
     for ref, at in ((low_ref, 0), (high_ref, HALO + rows)):
         left, right = ref[:HALO, :], ref[HALO : 2 * HALO, :]
@@ -415,20 +431,15 @@
         field[at : at + HALO, :] = jnp.where(lane < 64, pltpu.roll(left, 64, 1), pltpu.roll(right, 64, 1))
         at = at + FIELD_ROWS
         field[at : at + HALO, :] = right
-    rest = FIELD_ROWS - rows - 2 * HALO
-    for band in range(BANDS):
-        at = band * FIELD_ROWS + rows + 2 * HALO
-        field[at : at + rest, :] = jnp.zeros((rest, 128), f32)
     for q in range(10):
         at = q * SUP_PITCH
         sup[at : at + 3, :] = low_ref[2 * HALO + 4 * q + 1 : 2 * HALO + 4 * q + 4, :]
-        sup[at + 3 : at + 3 + blocks, :] = sup_ref[q]
         sup[at + 3 + blocks : at + 6 + blocks, :] = high_ref[2 * HALO + 4 * q : 2 * HALO + 4 * q + 3, :]
-        sup[at + 6 + blocks : at + SUP_PITCH, :] = jnp.zeros((SUP_PITCH - 6 - blocks, 128), f32)
+    turn_support(sup, turned)
     for copy in copies:
         copy.wait()
     build_cells(field, cells)
-    build_masks(cells, sup, turned, mask)
+    build_masks(cells, turned, mask)
     build_faces(cells, coef)
     iterate(functools.partial(first_vector, other, coef, mask), ITERS - 1)
     old, new = other, values
@@ -458,7 +469,7 @@
             pltpu.VMEM((9, HIGH, PITCH, 128), f32),
             pltpu.VMEM((LANE_PITCH * BLOCK_ROWS, 128), f32),
             pltpu.VMEM((blocks, 3, 2, 48, 128), f32),
-            pltpu.SemaphoreType.DMA((BANDS,)),
+            pltpu.SemaphoreType.DMA((4,)),
         ],
         compiler_params=pltpu.CompilerParams(vmem_limit_bytes=60 * 1024 * 1024),
         name="smooth",

time: 56.9 us -> 56.1 us (0.986)
  Pallas kernels: 36.1 us -> 35.4 us
    pallas_call x1, Pallas kernels: 29.2 us -> 28.4 us  [smooth(): pl.pallas_call(main_kernel, out_shape=jax.ShapeDtypeStruct((blocks, 3, 2,...]
where the time goes in v4:
time: 56.1 us; the launch traced here: 55.8 us
  Pallas kernels  35.4 us (63%)
  starting transfers between devices  12.1 us (22%)
  waiting for transfers between devices  7.04 us (13%)
  local copies, waits for them, and re-layouts  1.3 us (2%)
    pallas_call x1, Pallas kernels, smooth(): pl.pallas_call(main_kernel, out_shape=jax.ShapeDtypeStruct((blocks, 3, 2,...  28.4 us
    ppermute x4, starting transfers between devices, neighbours(): return (lax.ppermute(up, axis, forward), lax.ppermute(down, axis, backward))  12.1 us
    ppermute x4, waiting for transfers between devices, neighbours(): return (lax.ppermute(up, axis, forward), lax.ppermute(down, axis, backward))  7.04 us
    pallas_call x1, Pallas kernels, widen(): pl.pallas_call(widen_kernel, out_shape=(jax.ShapeDtypeStruct((BANDS, rows...  2.94 us
    pallas_call x1, Pallas kernels, pack(): pl.pallas_call(pack_kernel, out_shape=(shape, shape), name='pack')  2.06 us
    pallas_call x1, Pallas kernels, edges(): pl.pallas_call(edge_kernel, out_shape=(edge, edge), cost_estimate=cost(10...  1.93 us
    unnamed x8, local copies, waits for them, and re-layouts  1.3 us
  transfers between devices with their start and end apart: 4, of which 3 were waited for; matrix products, arithmetic and copies ran while one was open for 0% of the time, Pallas kernels for 5%

profile of v4, /device:TPU:1, one launch (start us, length us, event | category | flops | bytes accessed | tf_op | source)
XLA Modules:
  0.0 55.8 jit_solution(17825352477931334714)
XLA Ops:
  0.0 2.1 %pack.1 = (f32[376,128]{1,0:T(8,128)}, f32[376,128]{1,0:T(8,128)}) custom-call(f32[1024,128]{1,0:T(8,128)} %perm_ref.5, s32[32,4,36]{2,1,0:T(4,128)} %sup_ref.5), custom_call_target="tpu_custom_call" | custom-call | tf_op jit(solution)/shard_map/pack/pallas_call | solution.py:68
  2.1 4.0 %collective-permute-start = (f32[376,128]{1,0:T(8,128)}, f32[376,128]{1,0:T(8,128)S(1)}, u32[]{:S(2)}, u32[]{:S(2)}) collective-permute-start(f32[376,128]{1,0:T(8,128)} %get-tuple-element.11), channel_id=1, source_target_pairs={{0,1},{1,2},{2,3},{4,5},{5,6},{6,7},{8,9},{9,10},{10,11},{12,13},{... | collective-permute-start | bytes 577544 | tf_op jit(solution)/shard_map/ppermute | solution.py:483
  6.1 1.3 %collective-permute-start.1 = (f32[376,128]{1,0:T(8,128)}, f32[376,128]{1,0:T(8,128)S(1)}, u32[]{:S(2)}, u32[]{:S(2)}) collective-permute-start(f32[376,128]{1,0:T(8,128)} %get-tuple-element.12), channel_id=1, source_target_pairs={{1,0},{2,1},{3,2},{5,4},{6,5},{7,6},{9,8},{10,9},{11,10},{13,12},{... | collective-permute-start | bytes 577544 | tf_op jit(solution)/shard_map/ppermute | solution.py:483
  7.4 2.5 %collective-permute-done.left_ref = f32[376,128]{1,0:T(8,128)S(1)} collective-permute-done((f32[376,128]{1,0:T(8,128)}, f32[376,128]{1,0:T(8,128)S(1)}, u32[]{:S(2)}, u32[]{:S(2)}) %collective-permute-start) | collective-permute-done | bytes 192544 | tf_op jit(solution)/shard_map/ppermute | solution.py:483
  9.9 0.0 copy-start
  9.9 3.7 %collective-permute-done.1.right_ref = f32[376,128]{1,0:T(8,128)S(1)} collective-permute-done((f32[376,128]{1,0:T(8,128)}, f32[376,128]{1,0:T(8,128)S(1)}, u32[]{:S(2)}, u32[]{:S(2)}) %collective-permute-start.1) | collective-permute-done | bytes 192544 | tf_op jit(solution)/shard_map/ppermute | solution.py:483
  13.6 0.0 copy-done
  13.6 0.0 copy-start.1
  13.6 0.7 %copy-done.1 = f32[376,128]{1,0:T(8,128)} copy-done((f32[376,128]{1,0:T(8,128)}, f32[376,128]{1,0:T(8,128)S(1)}, u32[]{:S(2)}) %copy-start.1) | copy-done | bytes 192536
  14.2 1.9 %edges.1 = (f32[120,128]{1,0:T(8,128)}, f32[120,128]{1,0:T(8,128)}) custom-call(f32[1024,128]{1,0:T(8,128)} %perm_ref.5, s32[32,4,36]{2,1,0:T(4,128)} %sup_ref.5, f32[376,128]{1,0:T(8,128)} %copy-done, f32[376,128]{1,0:T(8,128)} %copy-done.1), custom_call_target="tpu_custom_call" | custom-call | flops 100000 | bytes 100000 | tf_op jit(solution)/shard_map/edges/pallas_call | solution.py:109
  16.2 4.9 %collective-permute-start.2 = (f32[120,128]{1,0:T(8,128)}, f32[120,128]{1,0:T(8,128)S(1)}, u32[]{:S(2)}, u32[]{:S(2)}) collective-permute-start(f32[120,128]{1,0:T(8,128)} %get-tuple-element.15), channel_id=1, source_target_pairs={{0,4},{4,8},{8,12},{1,5},{5,9},{9,13},{2,6},{6,10},{10,14},{3,7},{... | collective-permute-start | bytes 184328 | tf_op jit(solution)/shard_map/ppermute | solution.py:483
  21.0 1.9 %collective-permute-start.3 = (f32[120,128]{1,0:T(8,128)}, f32[120,128]{1,0:T(8,128)S(1)}, u32[]{:S(2)}, u32[]{:S(2)}) collective-permute-start(f32[120,128]{1,0:T(8,128)} %get-tuple-element.16), channel_id=1, source_target_pairs={{4,0},{8,4},{12,8},{5,1},{9,5},{13,9},{6,2},{10,6},{14,10},{7,3},{... | collective-permute-start | bytes 184328 | tf_op jit(solution)/shard_map/ppermute | solution.py:483
  23.0 2.9 %widen.1 = (f32[3,1024,128]{2,1,0:T(8,128)}, f32[10,32,128]{2,1,0:T(8,128)}) custom-call(f32[1024,128]{1,0:T(8,128)} %perm_ref.5, s32[32,4,36]{2,1,0:T(4,128)} %sup_ref.5, f32[376,128]{1,0:T(8,128)} %copy-done, f32[376,128]{1,0:T(8,128)} %copy-done.1), custom_call_target="tpu_custom_call" | custom-call | flops 4000000 | bytes 4000000 | tf_op jit(solution)/shard_map/widen/pallas_call | solution.py:130
  25.9 0.0 collective-permute-done.2.low_ref
  25.9 0.0 copy-start.2
  25.9 0.9 %collective-permute-done.3.high_ref = f32[120,128]{1,0:T(8,128)S(1)} collective-permute-done((f32[120,128]{1,0:T(8,128)}, f32[120,128]{1,0:T(8,128)S(1)}, u32[]{:S(2)}, u32[]{:S(2)}) %collective-permute-start.3) | collective-permute-done | bytes 61472 | tf_op jit(solution)/shard_map/ppermute | solution.py:483
  26.8 0.0 copy-start.3
  26.8 0.0 copy-done.2
  26.8 0.6 %copy-done.3 = f32[120,128]{1,0:T(8,128)} copy-done((f32[120,128]{1,0:T(8,128)}, f32[120,128]{1,0:T(8,128)S(1)}, u32[]{:S(2)}) %copy-start.3) | copy-done | bytes 61464
  27.4 28.4 %smooth.1 = f32[32,3,2,48,128]{4,3,2,1,0:T(8,128)} custom-call(f32[3,1024,128]{2,1,0:T(8,128)} %get-tuple-element.13.field_hbm, f32[10,32,128]{2,1,0:T(8,128)} %get-tuple-element.14.sup_ref, f32[120,128]{1,0:T(8,128)} %copy-done.2, f32[120,128]{1,0:T(8,128)} %copy-done.3), custom_call_target="tpu_custom_call" | custom-call | tf_op jit(solution)/shard_map/smooth/pallas_call | solution.py:456
Async XLA Ops:
  2.1 7.8 %collective-permute-start = (f32[376,128]{1,0:T(8,128)}, f32[376,128]{1,0:T(8,128)S(1)}, u32[]{:S(2)}, u32[]{:S(2)}) collective-permute-start(f32[376,128]{1,0:T(8,128)} %get-tuple-element.11), channel_id=1, source_target_pairs={{0,1},{1,2},{2,3},{4,5},{5,6},{6,7},{8,9},{9,10},{10,11},{12,13},{... | collective-permute-start | bytes 577544 | tf_op jit(solution)/shard_map/ppermute | solution.py:483
  6.1 7.5 %collective-permute-start.1 = (f32[376,128]{1,0:T(8,128)}, f32[376,128]{1,0:T(8,128)S(1)}, u32[]{:S(2)}, u32[]{:S(2)}) collective-permute-start(f32[376,128]{1,0:T(8,128)} %get-tuple-element.12), channel_id=1, source_target_pairs={{1,0},{2,1},{3,2},{5,4},{6,5},{7,6},{9,8},{10,9},{11,10},{13,12},{... | collective-permute-start | bytes 577544 | tf_op jit(solution)/shard_map/ppermute | solution.py:483
  9.9 3.7 %copy-start = (f32[376,128]{1,0:T(8,128)}, f32[376,128]{1,0:T(8,128)S(1)}, u32[]{:S(2)}) copy-start(f32[376,128]{1,0:T(8,128)S(1)} %collective-permute-done.left_ref) | copy-start | bytes 577540
  13.6 0.7 %copy-start.1 = (f32[376,128]{1,0:T(8,128)}, f32[376,128]{1,0:T(8,128)S(1)}, u32[]{:S(2)}) copy-start(f32[376,128]{1,0:T(8,128)S(1)} %collective-permute-done.1.right_ref) | copy-start | bytes 577540
  16.2 9.7 %collective-permute-start.2 = (f32[120,128]{1,0:T(8,128)}, f32[120,128]{1,0:T(8,128)S(1)}, u32[]{:S(2)}, u32[]{:S(2)}) collective-permute-start(f32[120,128]{1,0:T(8,128)} %get-tuple-element.15), channel_id=1, source_target_pairs={{0,4},{4,8},{8,12},{1,5},{5,9},{9,13},{2,6},{6,10},{10,14},{3,7},{... | collective-permute-start | bytes 184328 | tf_op jit(solution)/shard_map/ppermute | solution.py:483
  21.0 5.8 %collective-permute-start.3 = (f32[120,128]{1,0:T(8,128)}, f32[120,128]{1,0:T(8,128)S(1)}, u32[]{:S(2)}, u32[]{:S(2)}) collective-permute-start(f32[120,128]{1,0:T(8,128)} %get-tuple-element.16), channel_id=1, source_target_pairs={{4,0},{8,4},{12,8},{5,1},{9,5},{13,9},{6,2},{10,6},{14,10},{7,3},{... | collective-permute-start | bytes 184328 | tf_op jit(solution)/shard_map/ppermute | solution.py:483
  25.9 0.9 %copy-start.2 = (f32[120,128]{1,0:T(8,128)}, f32[120,128]{1,0:T(8,128)S(1)}, u32[]{:S(2)}) copy-start(f32[120,128]{1,0:T(8,128)S(1)} %collective-permute-done.2.low_ref) | copy-start | bytes 184324
  26.8 0.6 %copy-start.3 = (f32[120,128]{1,0:T(8,128)}, f32[120,128]{1,0:T(8,128)S(1)}, u32[]{:S(2)}) copy-start(f32[120,128]{1,0:T(8,128)S(1)} %collective-permute-done.3.high_ref) | copy-start | bytes 184324

commit v5 on v4

--- a/solution.py
+++ b/solution.py
@@ -459,7 +459,7 @@
         in_specs=[hbm, vmem, vmem, vmem],
         out_specs=hbm,
         scratch_shapes=[
-            pltpu.VMEM((BANDS * FIELD_ROWS, 128), f32),
+            pltpu.VMEM((BANDS * FIELD_ROWS + 32, 128), f32),
             pltpu.VMEM((10 * SUP_PITCH, 128), f32),
             pltpu.VMEM((HIGH, PITCH, 128), f32),
             pltpu.VMEM((5, 6, 40, 128), f32),
@@ -467,7 +467,7 @@
             pltpu.VMEM((4, HIGH, PITCH, 128), f32),
             pltpu.VMEM((9, HIGH, PITCH, 128), f32),
             pltpu.VMEM((9, HIGH, PITCH, 128), f32),
-            pltpu.VMEM((LANE_PITCH * BLOCK_ROWS, 128), f32),
+            pltpu.VMEM((LANE_PITCH * (BLOCK_ROWS + 1), 128), f32),
             pltpu.VMEM((blocks, 3, 2, 48, 128), f32),
             pltpu.SemaphoreType.DMA((4,)),
         ],

time: 56.1 us -> 56.1 us (level)
  no operation moved by 1% of the time
where the time goes in v5:
time: 56.1 us; the launch traced here: 55.8 us
  Pallas kernels  35.4 us (63%)
  starting transfers between devices  12.1 us (22%)
  waiting for transfers between devices  7.04 us (13%)
  local copies, waits for them, and re-layouts  1.3 us (2%)
    pallas_call x1, Pallas kernels, smooth(): pl.pallas_call(main_kernel, out_shape=jax.ShapeDtypeStruct((blocks, 3, 2,...  28.4 us
    ppermute x4, starting transfers between devices, neighbours(): return (lax.ppermute(up, axis, forward), lax.ppermute(down, axis, backward))  12.1 us
    ppermute x4, waiting for transfers between devices, neighbours(): return (lax.ppermute(up, axis, forward), lax.ppermute(down, axis, backward))  7.04 us
    pallas_call x1, Pallas kernels, widen(): pl.pallas_call(widen_kernel, out_shape=(jax.ShapeDtypeStruct((BANDS, rows...  2.94 us
    pallas_call x1, Pallas kernels, pack(): pl.pallas_call(pack_kernel, out_shape=(shape, shape), name='pack')  2.06 us
    pallas_call x1, Pallas kernels, edges(): pl.pallas_call(edge_kernel, out_shape=(edge, edge), cost_estimate=cost(10...  1.93 us
    unnamed x8, local copies, waits for them, and re-layouts  1.3 us
  transfers between devices with their start and end apart: 4, of which 3 were waited for; matrix products, arithmetic and copies ran while one was open for 0% of the time, Pallas kernels for 5%

profile of v5, /device:TPU:1, one launch (start us, length us, event | category | flops | bytes accessed | tf_op | source)
XLA Modules:
  0.0 55.8 jit_solution(12666601464913450822)
XLA Ops:
  0.0 2.1 %pack.1 = (f32[376,128]{1,0:T(8,128)}, f32[376,128]{1,0:T(8,128)}) custom-call(f32[1024,128]{1,0:T(8,128)} %perm_ref.5, s32[32,4,36]{2,1,0:T(4,128)} %sup_ref.5), custom_call_target="tpu_custom_call" | custom-call | tf_op jit(solution)/shard_map/pack/pallas_call | solution.py:68
  2.1 4.0 %collective-permute-start = (f32[376,128]{1,0:T(8,128)}, f32[376,128]{1,0:T(8,128)S(1)}, u32[]{:S(2)}, u32[]{:S(2)}) collective-permute-start(f32[376,128]{1,0:T(8,128)} %get-tuple-element.11), channel_id=1, source_target_pairs={{0,1},{1,2},{2,3},{4,5},{5,6},{6,7},{8,9},{9,10},{10,11},{12,13},{... | collective-permute-start | bytes 577544 | tf_op jit(solution)/shard_map/ppermute | solution.py:483
  6.1 1.3 %collective-permute-start.1 = (f32[376,128]{1,0:T(8,128)}, f32[376,128]{1,0:T(8,128)S(1)}, u32[]{:S(2)}, u32[]{:S(2)}) collective-permute-start(f32[376,128]{1,0:T(8,128)} %get-tuple-element.12), channel_id=1, source_target_pairs={{1,0},{2,1},{3,2},{5,4},{6,5},{7,6},{9,8},{10,9},{11,10},{13,12},{... | collective-permute-start | bytes 577544 | tf_op jit(solution)/shard_map/ppermute | solution.py:483
  7.4 2.5 %collective-permute-done.left_ref = f32[376,128]{1,0:T(8,128)S(1)} collective-permute-done((f32[376,128]{1,0:T(8,128)}, f32[376,128]{1,0:T(8,128)S(1)}, u32[]{:S(2)}, u32[]{:S(2)}) %collective-permute-start) | collective-permute-done | bytes 192544 | tf_op jit(solution)/shard_map/ppermute | solution.py:483
  9.9 0.0 copy-start
  9.9 3.7 %collective-permute-done.1.right_ref = f32[376,128]{1,0:T(8,128)S(1)} collective-permute-done((f32[376,128]{1,0:T(8,128)}, f32[376,128]{1,0:T(8,128)S(1)}, u32[]{:S(2)}, u32[]{:S(2)}) %collective-permute-start.1) | collective-permute-done | bytes 192544 | tf_op jit(solution)/shard_map/ppermute | solution.py:483
  13.6 0.0 copy-done
  13.6 0.0 copy-start.1
  13.6 0.7 %copy-done.1 = f32[376,128]{1,0:T(8,128)} copy-done((f32[376,128]{1,0:T(8,128)}, f32[376,128]{1,0:T(8,128)S(1)}, u32[]{:S(2)}) %copy-start.1) | copy-done | bytes 192536
  14.2 1.9 %edges.1 = (f32[120,128]{1,0:T(8,128)}, f32[120,128]{1,0:T(8,128)}) custom-call(f32[1024,128]{1,0:T(8,128)} %perm_ref.5, s32[32,4,36]{2,1,0:T(4,128)} %sup_ref.5, f32[376,128]{1,0:T(8,128)} %copy-done, f32[376,128]{1,0:T(8,128)} %copy-done.1), custom_call_target="tpu_custom_call" | custom-call | flops 100000 | bytes 100000 | tf_op jit(solution)/shard_map/edges/pallas_call | solution.py:109
  16.2 4.9 %collective-permute-start.2 = (f32[120,128]{1,0:T(8,128)}, f32[120,128]{1,0:T(8,128)S(1)}, u32[]{:S(2)}, u32[]{:S(2)}) collective-permute-start(f32[120,128]{1,0:T(8,128)} %get-tuple-element.15), channel_id=1, source_target_pairs={{0,4},{4,8},{8,12},{1,5},{5,9},{9,13},{2,6},{6,10},{10,14},{3,7},{... | collective-permute-start | bytes 184328 | tf_op jit(solution)/shard_map/ppermute | solution.py:483
  21.0 1.9 %collective-permute-start.3 = (f32[120,128]{1,0:T(8,128)}, f32[120,128]{1,0:T(8,128)S(1)}, u32[]{:S(2)}, u32[]{:S(2)}) collective-permute-start(f32[120,128]{1,0:T(8,128)} %get-tuple-element.16), channel_id=1, source_target_pairs={{4,0},{8,4},{12,8},{5,1},{9,5},{13,9},{6,2},{10,6},{14,10},{7,3},{... | collective-permute-start | bytes 184328 | tf_op jit(solution)/shard_map/ppermute | solution.py:483
  23.0 2.9 %widen.1 = (f32[3,1024,128]{2,1,0:T(8,128)}, f32[10,32,128]{2,1,0:T(8,128)}) custom-call(f32[1024,128]{1,0:T(8,128)} %perm_ref.5, s32[32,4,36]{2,1,0:T(4,128)} %sup_ref.5, f32[376,128]{1,0:T(8,128)} %copy-done, f32[376,128]{1,0:T(8,128)} %copy-done.1), custom_call_target="tpu_custom_call" | custom-call | flops 4000000 | bytes 4000000 | tf_op jit(solution)/shard_map/widen/pallas_call | solution.py:130
  25.9 0.0 collective-permute-done.2.low_ref
  25.9 0.0 copy-start.2
  25.9 0.9 %collective-permute-done.3.high_ref = f32[120,128]{1,0:T(8,128)S(1)} collective-permute-done((f32[120,128]{1,0:T(8,128)}, f32[120,128]{1,0:T(8,128)S(1)}, u32[]{:S(2)}, u32[]{:S(2)}) %collective-permute-start.3) | collective-permute-done | bytes 61472 | tf_op jit(solution)/shard_map/ppermute | solution.py:483
  26.8 0.0 copy-start.3
  26.8 0.0 copy-done.2
  26.8 0.6 %copy-done.3 = f32[120,128]{1,0:T(8,128)} copy-done((f32[120,128]{1,0:T(8,128)}, f32[120,128]{1,0:T(8,128)S(1)}, u32[]{:S(2)}) %copy-start.3) | copy-done | bytes 61464
  27.4 28.4 %smooth.1 = f32[32,3,2,48,128]{4,3,2,1,0:T(8,128)} custom-call(f32[3,1024,128]{2,1,0:T(8,128)} %get-tuple-element.13.field_hbm, f32[10,32,128]{2,1,0:T(8,128)} %get-tuple-element.14.sup_ref, f32[120,128]{1,0:T(8,128)} %copy-done.2, f32[120,128]{1,0:T(8,128)} %copy-done.3), custom_call_target="tpu_custom_call" | custom-call | tf_op jit(solution)/shard_map/smooth/pallas_call | solution.py:456
Async XLA Ops:
  2.1 7.8 %collective-permute-start = (f32[376,128]{1,0:T(8,128)}, f32[376,128]{1,0:T(8,128)S(1)}, u32[]{:S(2)}, u32[]{:S(2)}) collective-permute-start(f32[376,128]{1,0:T(8,128)} %get-tuple-element.11), channel_id=1, source_target_pairs={{0,1},{1,2},{2,3},{4,5},{5,6},{6,7},{8,9},{9,10},{10,11},{12,13},{... | collective-permute-start | bytes 577544 | tf_op jit(solution)/shard_map/ppermute | solution.py:483
  6.1 7.5 %collective-permute-start.1 = (f32[376,128]{1,0:T(8,128)}, f32[376,128]{1,0:T(8,128)S(1)}, u32[]{:S(2)}, u32[]{:S(2)}) collective-permute-start(f32[376,128]{1,0:T(8,128)} %get-tuple-element.12), channel_id=1, source_target_pairs={{1,0},{2,1},{3,2},{5,4},{6,5},{7,6},{9,8},{10,9},{11,10},{13,12},{... | collective-permute-start | bytes 577544 | tf_op jit(solution)/shard_map/ppermute | solution.py:483
  9.9 3.7 %copy-start = (f32[376,128]{1,0:T(8,128)}, f32[376,128]{1,0:T(8,128)S(1)}, u32[]{:S(2)}) copy-start(f32[376,128]{1,0:T(8,128)S(1)} %collective-permute-done.left_ref) | copy-start | bytes 577540
  13.6 0.7 %copy-start.1 = (f32[376,128]{1,0:T(8,128)}, f32[376,128]{1,0:T(8,128)S(1)}, u32[]{:S(2)}) copy-start(f32[376,128]{1,0:T(8,128)S(1)} %collective-permute-done.1.right_ref) | copy-start | bytes 577540
  16.2 9.7 %collective-permute-start.2 = (f32[120,128]{1,0:T(8,128)}, f32[120,128]{1,0:T(8,128)S(1)}, u32[]{:S(2)}, u32[]{:S(2)}) collective-permute-start(f32[120,128]{1,0:T(8,128)} %get-tuple-element.15), channel_id=1, source_target_pairs={{0,4},{4,8},{8,12},{1,5},{5,9},{9,13},{2,6},{6,10},{10,14},{3,7},{... | collective-permute-start | bytes 184328 | tf_op jit(solution)/shard_map/ppermute | solution.py:483
  21.0 5.8 %collective-permute-start.3 = (f32[120,128]{1,0:T(8,128)}, f32[120,128]{1,0:T(8,128)S(1)}, u32[]{:S(2)}, u32[]{:S(2)}) collective-permute-start(f32[120,128]{1,0:T(8,128)} %get-tuple-element.16), channel_id=1, source_target_pairs={{4,0},{8,4},{12,8},{5,1},{9,5},{13,9},{6,2},{10,6},{14,10},{7,3},{... | collective-permute-start | bytes 184328 | tf_op jit(solution)/shard_map/ppermute | solution.py:483
  25.9 0.9 %copy-start.2 = (f32[120,128]{1,0:T(8,128)}, f32[120,128]{1,0:T(8,128)S(1)}, u32[]{:S(2)}) copy-start(f32[120,128]{1,0:T(8,128)S(1)} %collective-permute-done.2.low_ref) | copy-start | bytes 184324
  26.8 0.6 %copy-start.3 = (f32[120,128]{1,0:T(8,128)}, f32[120,128]{1,0:T(8,128)S(1)}, u32[]{:S(2)}) copy-start(f32[120,128]{1,0:T(8,128)S(1)} %collective-permute-done.3.high_ref) | copy-start | bytes 184324
